TPU v7x, 32 devices: a whole 2x2x4 slice. The times are simulated.
32 devices in a mesh: pix: 16 (over z, y, x), mode: 2 (over core).
Axes of the slice: x: 2, y: 2, z: 4, core: 2. Of those that a mesh axis runs over, the one named last changes fastest.
Arguments:
- frames: bfloat16 [4, 8192, 2048], P(None, 'pix', 'mode'), may hold values from 0 to 4
- ref_pixels: int32 [64], replicated, may hold values from 0 to 8191
Outputs:
- gram_band: float32 [2, 2048, 1024], P(None, 'mode', 'pix')
- gram_diag: float32 [2, 2048, 1024], P(None, 'mode', 'pix')
Inputs may be any that keep to these rules, and one draw needn't show every extreme that they name: `ref_pixels`: indices of reference pixels; an index may appear more than once.
All inputs are finite; a program needn't handle non-finite values.
Results may differ from a plain program's by a relative error of at most 0.0088.
Values may be sent and summed in bfloat16 or wider, within the bound.
A program may use at most 128 MiB of HBM per device.

v0:
```python
import math

import jax
import jax.numpy as jnp
from jax import lax
from jax.sharding import PartitionSpec as P


def unit_phase(sums):
    magnitude = jnp.maximum(jnp.sqrt(sums[0] * sums[0] + sums[1] * sums[1]), 1.0)
    return sums / magnitude[None, :]


def rotate(gram_real, gram_imag, phase_rows, phase_cols, pixel_scale):
    row_real = phase_rows[0][:, None]
    row_imag = phase_rows[1][:, None]
    col_real = phase_cols[0][None, :]
    col_imag = phase_cols[1][None, :]
    unit_real = row_real * col_real + row_imag * col_imag
    unit_imag = row_imag * col_real - row_real * col_imag
    return jnp.stack(
        [
            (unit_real * gram_real - unit_imag * gram_imag) * pixel_scale,
            (unit_real * gram_imag + unit_imag * gram_real) * pixel_scale,
        ]
    )


def shards(frames, ref_pixels):
    pix_count = lax.axis_size("pix")
    mode_count = lax.axis_size("mode")
    pix_index = lax.axis_index("pix")
    mode_index = lax.axis_index("mode")
    pixel_rows = frames.shape[1]
    block_width = frames.shape[2]
    full_tiles = mode_count // 2 + 1
    full_width = full_tiles * block_width
    frame_float = frames.astype(jnp.float32)
    real_part = (frame_float[0] - frame_float[2]).astype(jnp.bfloat16)
    imag_part = (frame_float[3] - frame_float[1]).astype(jnp.bfloat16)
    fields = jnp.stack([real_part, imag_part])
    positions = pix_index * pixel_rows + lax.iota(jnp.int32, pixel_rows)
    counts = jnp.sum(
        (ref_pixels[:, None] == positions[None, :]).astype(jnp.float32), axis=0
    ).astype(jnp.bfloat16)
    local_ref = jnp.einsum("p,cpm->cm", counts, fields, preferred_element_type=jnp.float32)
    own_ref = lax.psum(local_ref, "pix")
    phase_all = lax.all_gather(unit_phase(own_ref), "mode", axis=1, tiled=True)
    phase_own = lax.dynamic_slice_in_dim(phase_all, mode_index * block_width, block_width, 1)
    phase_twice = jnp.concatenate([phase_all, phase_all], axis=1)
    phase_full = lax.dynamic_slice_in_dim(phase_twice, mode_index * block_width, full_width, 1)
    whole_fields = lax.all_gather(fields, "mode", axis=2, tiled=True)
    tiled = whole_fields.reshape(2, pixel_rows, mode_count, block_width)
    picked = (mode_index + lax.iota(jnp.int32, full_tiles)) % mode_count
    band_fields = jnp.take(tiled, picked, axis=2).reshape(2, pixel_rows, full_width)
    contract = (((0,), (0,)), ((), ()))
    own_real = fields[0]
    own_imag = fields[1]
    band_real = band_fields[0]
    band_imag = band_fields[1]
    gram_real = lax.dot_general(
        own_real, band_real, contract, preferred_element_type=jnp.float32
    ) + lax.dot_general(own_imag, band_imag, contract, preferred_element_type=jnp.float32)
    gram_imag = lax.dot_general(
        own_real, band_imag, contract, preferred_element_type=jnp.float32
    ) - lax.dot_general(own_imag, band_real, contract, preferred_element_type=jnp.float32)
    pixel_scale = 1.0 / math.sqrt(pix_count * pixel_rows)
    raw_terms = jnp.stack([gram_real, gram_imag])
    raw_diag, raw_band = (
        lax.psum_scatter(raw_terms[:, :, :block_width], "pix", scatter_dimension=2, tiled=True),
        lax.psum_scatter(raw_terms[:, :, block_width:], "pix", scatter_dimension=2, tiled=True),
    )
    diag_slice = block_width // pix_count
    band_slice = (full_width - block_width) // pix_count
    diag_cols = lax.dynamic_slice_in_dim(phase_full, pix_index * diag_slice, diag_slice, 1)
    band_cols = lax.dynamic_slice_in_dim(
        phase_full, block_width + pix_index * band_slice, band_slice, 1
    )
    diag_out = rotate(raw_diag[0], raw_diag[1], phase_own, diag_cols, pixel_scale)
    band_out = rotate(raw_band[0], raw_band[1], phase_own, band_cols, pixel_scale)
    return (band_out, diag_out)


def solution(mesh):
    placed = (P(None, "pix", "mode"), P())
    return jax.shard_map(
        shards,
        mesh=mesh,
        in_specs=placed,
        out_specs=(P(None, "mode", "pix"), P(None, "mode", "pix")),
        check_vma=False,
    )
```

profile of v0, /device:TPU:0, one launch (start us, length us, event | category | flops | bytes accessed | tf_op | source)
XLA Modules:
  0.0 582.5 jit_solution(13242077597247276007)
XLA Ops:
  7.2 0.0 all-gather.2.cloned.1.call-start
  7.2 6.3 %copy.33 = bf16[4,512,1024]{1,2,0:T(8,128)(2,1)} copy(bf16[4,512,1024]{2,1,0:T(8,128)(2,1)} %param.2) | data formatting | bytes 8388608 | tf_op args[0]
  13.5 3.4 convert_element_type.27
  16.8 0.9 fusion.2
  17.7 0.0 copy-start.2
  17.7 1.1 copy-done.2
  18.8 1.5 pad_maximum_fusion.1
  20.3 0.0 all-gather.2.cloned.1.call-update
  20.3 0.0 all-reduce.5.cloned.1.call-start
  20.4 16.4 %all-gather.2.cloned.1.call-done = bf16[2,512,2048]{1,2,0:T(8,128)(2,1)} async-done(((bf16[2,512,1024]{1,2,0:T(8,128)(2,1)}), bf16[2,512,2048]{1,2,0:T(8,128)(2,1)}) %all-gather.2.cloned.1.call-update) | async-done | bytes 4194320 | tf_op jit(solution)/shard_map/all_gather | solution.py:52
  36.8 4.5 fusion.14
  41.3 2.8 copy.45
  44.1 4.2 copy.46
  48.3 2.0 gather_fusion
  50.3 3.7 gather_fusion.1
  54.1 0.0 copy-done.1
  54.1 2.6 maximum_select_fusion
  56.7 1.8 fusion.13
  58.5 4.0 copy.37
  62.5 2.6 copy.36
  65.1 4.4 fusion.7
  69.5 0.0 copy-done.3
  69.5 0.0 copy-done.5
  69.5 2.4 fusion.5
  71.9 0.0 copy-start.4
  71.9 2.6 add_bitcast_fusion
  74.5 0.0 copy-done.4
  74.5 2.4 subtract_bitcast_fusion
  76.9 6.6 %pad_maximum_fusion = (f32[2,1024,1024]{2,1,0:T(8,128)}, f32[2,1024,1024]{2,1,0:T(8,128)}) fusion(f32[1,1024,2048]{2,1,0:T(8,128)S(1)} %subtract_bitcast_fusion, f32[1,1024,2048]{2,1,0:T(8,128)S(1)} %add_bitcast_fusion), kind=kLoop, calls=%fused_computation.5 | loop fusion | flops 4194304 | bytes 33554432 | tf_op jit(solution)/shard_map/stack | solution.py:68
  83.6 13.4 %copy.41 = f32[2,1024,1024]{1,0,2:T(2,128)} copy(f32[2,1024,1024]{2,1,0:T(8,128)} %get-tuple-element.14) | data formatting | bytes 16777216 | tf_op jit(solution)/shard_map/slice | solution.py:70
  97.0 13.3 %copy.38 = f32[2,1024,1024]{1,0,2:T(2,128)} copy(f32[2,1024,1024]{2,1,0:T(8,128)} %get-tuple-element.15) | data formatting | bytes 16777216 | tf_op jit(solution)/shard_map/slice | solution.py:71
  110.3 0.0 all-reduce.5.cloned.1.call-update
  110.3 0.0 copy-start.7
  110.4 0.6 copy-done.6
  110.9 0.1 convert_reduce_fusion
  111.0 0.8 copy-done
  111.9 0.6 fusion.15
  112.5 0.0 copy-done.7
  112.6 0.6 dynamic-slice
  113.8 45.2 %psum.7 = f32[2,1024]{1,0:T(2,128)S(1)} all-reduce(f32[2,1024]{1,0:T(2,128)S(1)} %bitcast.49), channel_id=1, replica_groups=mesh['pix'=16,'mode'=2] {'pix'}, use_global_device_ids=true, to_apply=%region_1.0 | all-reduce | flops 2048 | bytes 16384 | tf_op jit(solution)/shard_map/psum | solution.py:47
  159.1 1.8 all_gather.6
  160.9 0.1 constant_dynamic-slice_fusion.5
  161.0 0.1 constant_dynamic-slice_fusion.4
  161.1 410.1 %all-reduce.5.cloned.1.call-done = (f32[2,1024,1024]{1,0,2:T(2,128)}, f32[2,1024,1024]{1,0,2:T(2,128)}) async-done(((f32[2,1024,1024]{1,0,2:T(2,128)}, f32[2,1024,1024]{1,0,2:T(2,128)}), (f32[2,1024,1024]{1,0,2:T(2,128)}, f32[2,1024,1024]{1,0,2:T(2,128)})) %all-reduce.5.cloned.1.call-update) | async-done | bytes 16777232
  571.2 2.4 constant_dynamic-slice_fusion
  573.6 0.4 subtract_multiply_fusion
  574.0 0.8 pad_maximum_fusion.3
  574.8 0.8 pad_maximum_fusion.2
  (16 shorter events, 0.1 us)
Async XLA Ops:
  7.2 29.7 %all-gather.2.cloned.1.call-start = ((), (), s32[]{:S(2)}) async-start(), calls=%async_computation | async-start | bytes 6291456 | tf_op jit(solution)/shard_map/all_gather | solution.py:52
  17.7 1.1 copy-start.2
  20.3 550.9 %all-reduce.5.cloned.1.call-start = ((), (), s32[]{:S(2)}) async-start(), calls=%async_computation.1 | async-start | bytes 33554432
  50.3 3.8 copy-start.1
  65.1 4.4 copy-start.3
  65.1 4.4 copy-start.5
  71.9 2.6 copy-start.4
  110.3 0.7 copy-start.6
  110.3 1.6 copy-start
  110.3 2.2 copy-start.7
Sparse Core Ops, SparseCore 0:
  20.4 16.3 all-gather.1
  110.4 460.7 all-reduce.4
where the time goes:
time: 584 us; the launch traced here: 583 us
  waiting for transfers between devices  427 us (73%)
  local copies, waits for them, and re-layouts  64.3 us (11%)
  blocking collectives  47 us (8%)
  other arithmetic  17.2 us (3%)
  between operations  14.9 us (3%)
  matrix products  12.4 us (2%)
    unnamed x3, waiting for transfers between devices  410 us
    psum x1, blocking collectives, shards(): own_ref = lax.psum(local_ref, 'pix')  45.2 us
    all_gather x1, waiting for transfers between devices, shards(): whole_fields = lax.all_gather(fields, 'mode', axis=2, tiled=True)  16.4 us
    unnamed x21, local copies, waits for them, and re-layouts  16.3 us
    slice x1, local copies, waits for them, and re-layouts, shards(): raw_terms[:, :, :block_width]  13.4 us
    slice x1, local copies, waits for them, and re-layouts, shards(): raw_terms[:, :, block_width:]  13.3 us
  transfers between devices with their start and end apart: 2, of which 2 were waited for; matrix products, arithmetic and copies ran while one was open for 0% of the time, Pallas kernels for 0%

commit v1 on v0

--- a/solution.py
+++ b/solution.py
@@ -3,6 +3,8 @@
 import jax
 import jax.numpy as jnp
 from jax import lax
+from jax.experimental import pallas as pl
+from jax.experimental.pallas import tpu as pltpu
 from jax.sharding import PartitionSpec as P
 
 
@@ -81,10 +83,379 @@
     return (band_out, diag_out)
 
 
+MESH = pl.DeviceIdType.MESH
+GROUP = 64
+NEAR = 9
+FAR = 7
+
+
+def gram_kernel(
+    frames_ref, weight_ref, gram_ref, sums_ref,
+    own, other, part, first_in, second_in, outer_in, inner_in, end_in,
+    ref_out, ref_in, total, cross_out, cross_in, turn_out, turn_in,
+    field_send, field_recv, first_send, first_recv, second_send, second_recv,
+    line_send, outer_recv, inner_recv, end_recv, ref_send, ref_recv,
+    cross_send, cross_recv, turn_send, turn_recv,
+):
+    pix = lax.axis_index("pix")
+    mode = lax.axis_index("mode")
+    x, y, z = pix % 2, (pix // 2) % 2, pix // 4
+    upper = z >= 2
+    is_end = (z == 0) | (z == 3)
+    is_mid = (z == 1) | (z == 2)
+    x_peer = pix + 1 - 2 * x
+    y_peer = pix + 2 - 4 * y
+    inner_peer = jnp.where(upper, pix - 4, pix + 4)
+    outer_peer = jnp.where(upper, pix + 4, pix - 4)
+    z_even_peer = pix + 4 - 8 * (z % 2)
+    z_far_peer = pix + 8 - 16 * (z // 2)
+    pixel_rows = frames_ref.shape[1]
+    width = frames_ref.shape[2]
+    rows = NEAR * GROUP
+    half = rows // 2
+    chunk = 4 * GROUP
+
+    barrier = pltpu.get_barrier_semaphore()
+    for step in range(1, 16):
+        pl.semaphore_signal(
+            barrier, inc=1, device_id=((pix + step) % 16, mode), device_id_type=MESH
+        )
+    pl.semaphore_signal(barrier, inc=1, device_id=(pix, 1 - mode), device_id_type=MESH)
+
+    def send(src, dst, send_sem, recv_sem, to_pix, to_mode):
+        copy = pltpu.make_async_remote_copy(
+            src_ref=src, dst_ref=dst, send_sem=send_sem, recv_sem=recv_sem,
+            device_id=(to_pix, to_mode), device_id_type=MESH,
+        )
+        return copy
+
+    def chunk_z(k):
+        return jnp.where(upper, k, 3 - k)
+
+    def field_chunk(k, carry):
+        at = pl.multiple_of(chunk_z(k) * chunk, chunk)
+        cols = pl.ds(at, chunk)
+        real = frames_ref[0, :, cols].astype(jnp.float32) - frames_ref[2, :, cols].astype(jnp.float32)
+        imag = frames_ref[3, :, cols].astype(jnp.float32) - frames_ref[1, :, cols].astype(jnp.float32)
+        own[cols, 0:pixel_rows] = real.astype(jnp.bfloat16).T
+        own[cols, pixel_rows:2 * pixel_rows] = imag.astype(jnp.bfloat16).T
+        return carry
+
+    lax.fori_loop(0, 4, field_chunk, 0)
+    own[pl.ds(width, 8 * GROUP), :] = own[pl.ds(0, 8 * GROUP), :]
+    pl.semaphore_wait(barrier, 16)
+
+    def field_copy(k):
+        cols = pl.ds(pl.multiple_of(chunk_z(k) * chunk, chunk), chunk)
+        return send(own.at[cols], other.at[cols], field_send.at[k], field_recv.at[k], pix, 1 - mode)
+
+    field_copies = [field_copy(k) for k in range(4)]
+    for copy in field_copies:
+        copy.start()
+
+    ref_peers = [x_peer, y_peer, z_even_peer, z_far_peer, pix]
+
+    def ref_copy(step):
+        return send(
+            ref_out.at[step], ref_in.at[step], ref_send.at[step], ref_recv.at[step],
+            ref_peers[step], mode if step < 4 else 1 - mode,
+        )
+
+    ref_copies = [ref_copy(step) for step in range(5)]
+
+    def ref_next(step):
+        ref_copies[step].wait_recv()
+        ref_out[step + 1] = ref_out[step] + ref_in[step]
+        ref_copies[step + 1].start()
+
+    contract = (((1,), (1,)), ((), ()))
+
+    def turned(block):
+        return jnp.concatenate([block[:, pixel_rows:], -block[:, :pixel_rows]], axis=1)
+
+    def multiply(k):
+        zc = chunk_z(k)
+        field_copies[k].wait_recv()
+
+        def one(t, carry):
+            yy = jnp.where(t % 2 == 0, 1 - y, y)
+            xx = jnp.where(t < 2, 1 - x, x)
+            owner = zc * 4 + yy * 2 + xx
+            at = pl.multiple_of(owner * GROUP, GROUP)
+            own_cols = own[pl.ds(at, GROUP), :]
+            other_cols = other[pl.ds(at, GROUP), :]
+            cols = jnp.concatenate(
+                [own_cols, turned(own_cols), other_cols, turned(other_cols)], axis=0
+            )
+            left = own[pl.ds(at, rows), :]
+            out = lax.dot_general(left, cols, contract, preferred_element_type=jnp.float32)
+            part[owner] = out.astype(jnp.bfloat16)
+            return carry
+
+        lax.fori_loop(0, 4, one, 0)
+
+    spans = [pl.ds(0, half), pl.ds(half, half)]
+
+    def owner_of(k, yy, xx):
+        return chunk_z(k) * 4 + yy * 2 + xx
+
+    def first_copy(axis, k, j):
+        if axis == 0:
+            owner = owner_of(k, 1 - y if j == 0 else y, 1 - x)
+        else:
+            owner = owner_of(k, 1 - y, 1 - x if j == 0 else x)
+        return send(
+            part.at[owner, spans[axis]], first_in.at[axis, k, j],
+            first_send.at[axis, k, j], first_recv.at[axis, k, j],
+            x_peer if axis == 0 else y_peer, mode,
+        )
+
+    def second_owner(axis, k):
+        return owner_of(k, 1 - y, x) if axis == 0 else owner_of(k, y, 1 - x)
+
+    def second_copy(axis, k):
+        return send(
+            part.at[second_owner(axis, k), spans[axis]], second_in.at[axis, k],
+            second_send.at[axis, k], second_recv.at[axis, k],
+            y_peer if axis == 0 else x_peer, mode,
+        )
+
+    firsts = {(a, k, j): first_copy(a, k, j) for a in range(2) for k in range(4) for j in range(2)}
+    seconds = {(a, k): second_copy(a, k) for a in range(2) for k in range(4)}
+
+    def f32(value):
+        return value.astype(jnp.float32)
+
+    def begin(k):
+        multiply(k)
+        for j in range(2):
+            for a in range(2):
+                firsts[a, k, j].start()
+
+    def forward(k):
+        for a in range(2):
+            firsts[a, k, 0].wait_recv()
+            owner = second_owner(a, k)
+            part[owner, spans[a]] = (
+                f32(part[owner, spans[a]]) + f32(first_in[a, k, 0])
+            ).astype(jnp.bfloat16)
+            seconds[a, k].start()
+
+    def line_copy(k, to):
+        owner = owner_of(k, y, x)
+        if to == "outer":
+            dst, sem = outer_in.at[k], outer_recv.at[k]
+        elif to == "inner":
+            dst, sem = inner_in.at[k], inner_recv.at[k]
+        else:
+            dst, sem = end_in, end_recv
+        return send(
+            part.at[owner], dst, line_send.at[k], sem,
+            outer_peer if to == "end" else inner_peer, mode,
+        )
+
+    def keep(k):
+        owner = owner_of(k, y, x)
+        for a in range(2):
+            firsts[a, k, 1].wait_recv()
+            seconds[a, k].wait_recv()
+            value = (
+                f32(part[owner, spans[a]]) + f32(first_in[a, k, 1]) + f32(second_in[a, k])
+            )
+            if k >= 2:
+                @pl.when(is_mid if k == 2 else is_end)
+                def _():
+                    total[spans[a], :] = value
+            part[owner, spans[a]] = value.astype(jnp.bfloat16)
+        if k < 3:
+            @pl.when(is_end)
+            def _():
+                line_copy(k, "outer").start()
+
+    def pass_on(k):
+        owner = owner_of(k, y, x)
+
+        @pl.when(is_mid)
+        def _():
+            if k < 2:
+                line_copy(k, "outer").wait_recv()
+                arrived = outer_in[k]
+            else:
+                line_copy(0, "inner").wait_recv()
+                arrived = inner_in[0]
+            part[owner] = (f32(part[owner]) + f32(arrived)).astype(jnp.bfloat16)
+            line_copy(k, "inner" if k < 2 else "end").start()
+
+    begin(0)
+    begin(1)
+    ref_out[0] = lax.dot_general(
+        weight_ref[...], own[pl.ds(0, width), :], contract, preferred_element_type=jnp.float32
+    )[0:8]
+    ref_copies[0].start()
+    forward(0)
+    begin(2)
+    ref_next(0)
+    forward(1)
+    keep(0)
+    begin(3)
+    ref_next(1)
+    forward(2)
+    keep(1)
+    pass_on(0)
+    ref_next(2)
+    forward(3)
+    keep(2)
+    pass_on(1)
+    ref_next(3)
+    keep(3)
+    pass_on(3)
+
+    @pl.when(is_mid)
+    def _():
+        line_copy(2, "outer").wait_recv()
+        line_copy(1, "inner").wait_recv()
+        total[...] = total[...] + f32(outer_in[2]) + f32(inner_in[1])
+
+    @pl.when(is_end)
+    def _():
+        line_copy(3, "end").wait_recv()
+        total[...] = total[...] + f32(end_in[...])
+
+    cross_out[...] = total[GROUP:8 * GROUP, 128:256].astype(jnp.bfloat16)
+    cross = send(cross_out, cross_in, cross_send, cross_recv, pix, 1 - mode)
+    cross.start()
+
+    lane = lax.broadcasted_iota(jnp.int32, (GROUP, 128), 1)
+    low = lane < GROUP
+
+    def group_rows(step):
+        return pl.ds(pl.multiple_of(((pix + step) % 16) * GROUP, GROUP), GROUP)
+
+    for d in range(NEAR):
+        here = total[d * GROUP:(d + 1) * GROUP, 0:128]
+        there = total[d * GROUP:(d + 1) * GROUP, 128:256]
+        gram_ref[0, group_rows(d), :] = jnp.where(low, here, pltpu.roll(there, GROUP, 1))
+        gram_ref[1, group_rows(d), :] = jnp.where(low, pltpu.roll(here, GROUP, 1), there)
+
+    cross.wait_recv()
+    turns = []
+    for d in range(1, FAR + 1):
+        stacked = jnp.concatenate(
+            [
+                total[d * GROUP:(d + 1) * GROUP, 0:128].astype(jnp.bfloat16),
+                cross_in[(d - 1) * GROUP:d * GROUP, :],
+            ],
+            axis=0,
+        )
+        turn_out[d - 1] = stacked.T
+        turn = send(
+            turn_out.at[d - 1], turn_in.at[d - 1], turn_send.at[d - 1], turn_recv.at[d - 1],
+            (pix + d) % 16, mode,
+        )
+        turn.start()
+        turns.append(turn)
+    ref_copies[4].wait_recv()
+    sums_ref[0] = ref_out[4]
+    sums_ref[1] = ref_in[4]
+    for d in range(1, FAR + 1):
+        turns[d - 1].wait_recv()
+        arrived = f32(turn_in[d - 1])
+        gram_ref[0, group_rows(16 - d), :] = arrived[0:GROUP]
+        gram_ref[1, group_rows(16 - d), :] = -arrived[GROUP:]
+
+    for copy in field_copies + ref_copies + list(firsts.values()) + list(seconds.values()):
+        copy.wait_send()
+    for copy in turns + [cross]:
+        copy.wait_send()
+    for k in range(3):
+        @pl.when(is_end | (k < 2))
+        def _():
+            line_copy(k, "outer").wait_send()
+
+    @pl.when(is_mid)
+    def _():
+        line_copy(3, "end").wait_send()
+
+
+def paired_shards(frames, ref_pixels):
+    pix_index = lax.axis_index("pix")
+    pixel_rows = frames.shape[1]
+    width = frames.shape[2]
+    positions = pix_index * pixel_rows + lax.iota(jnp.int32, pixel_rows)
+    counts = jnp.sum(
+        (ref_pixels[:, None] == positions[None, :]).astype(jnp.float32), axis=0
+    ).astype(jnp.bfloat16)
+    weight = (
+        jnp.zeros((16, 2 * pixel_rows), jnp.bfloat16)
+        .at[0, :pixel_rows].set(counts)
+        .at[1, pixel_rows:].set(counts)
+    )
+    rows = NEAR * GROUP
+    half = rows // 2
+    b16 = jnp.bfloat16
+    dma = pltpu.SemaphoreType.DMA
+    gram, sums = pl.pallas_call(
+        gram_kernel,
+        out_shape=(
+            jax.ShapeDtypeStruct((2, width, 128), jnp.float32),
+            jax.ShapeDtypeStruct((2, 8, width), jnp.float32),
+        ),
+        in_specs=[pl.BlockSpec(memory_space=pltpu.VMEM)] * 2,
+        out_specs=(pl.BlockSpec(memory_space=pltpu.VMEM),) * 2,
+        scratch_shapes=[
+            pltpu.VMEM((width + 8 * GROUP, 2 * pixel_rows), b16),
+            pltpu.VMEM((width, 2 * pixel_rows), b16),
+            pltpu.VMEM((16, rows, 256), b16),
+            pltpu.VMEM((2, 4, 2, half, 256), b16),
+            pltpu.VMEM((2, 4, half, 256), b16),
+            pltpu.VMEM((3, rows, 256), b16),
+            pltpu.VMEM((2, rows, 256), b16),
+            pltpu.VMEM((rows, 256), b16),
+            pltpu.VMEM((5, 8, width), jnp.float32),
+            pltpu.VMEM((5, 8, width), jnp.float32),
+            pltpu.VMEM((rows, 256), jnp.float32),
+            pltpu.VMEM((FAR * GROUP, 128), b16),
+            pltpu.VMEM((FAR * GROUP, 128), b16),
+            pltpu.VMEM((FAR, 128, 128), b16),
+            pltpu.VMEM((FAR, 128, 128), b16),
+            dma((4,)), dma((4,)),
+            dma((2, 4, 2)), dma((2, 4, 2)),
+            dma((2, 4)), dma((2, 4)),
+            dma((4,)), dma((3,)), dma((2,)), dma,
+            dma((5,)), dma((5,)),
+            dma, dma,
+            dma((FAR,)), dma((FAR,)),
+        ],
+        compiler_params=pltpu.CompilerParams(
+            collective_id=0, has_side_effects=True, vmem_limit_bytes=48 * 1024 * 1024
+        ),
+    )(frames, weight)
+    phase_own = unit_phase(sums[0, :2])
+    phase_other = unit_phase(sums[1, :2])
+    start = pix_index * GROUP
+    cols = jnp.concatenate(
+        [
+            lax.dynamic_slice_in_dim(phase_own, start, GROUP, 1),
+            lax.dynamic_slice_in_dim(phase_other, start, GROUP, 1),
+        ],
+        axis=1,
+    )
+    pixel_scale = 1.0 / math.sqrt(lax.axis_size("pix") * pixel_rows)
+    turned = rotate(gram[0], gram[1], phase_own, cols, pixel_scale)
+    return (turned[:, :, GROUP:], turned[:, :, :GROUP])
+
+
 def solution(mesh):
     placed = (P(None, "pix", "mode"), P())
+    paired = mesh.shape["pix"] == 16 and mesh.shape["mode"] == 2
+
+    def body(frames, ref_pixels):
+        if paired and frames.shape[2] == 16 * GROUP:
+            return paired_shards(frames, ref_pixels)
+        return shards(frames, ref_pixels)
+
     return jax.shard_map(
-        shards,
+        body,
         mesh=mesh,
         in_specs=placed,
         out_specs=(P(None, "mode", "pix"), P(None, "mode", "pix")),

time: 584 us -> 73.6 us (0.13)
  waiting for transfers between devices: 427 us -> 0 us
  Pallas kernels: 0 us -> 65.7 us
  local copies, waits for them, and re-layouts: 64.3 us -> 4.74 us
  blocking collectives: 47 us -> 0 us
  other arithmetic: 17.2 us -> 1.63 us
  between operations: 14.9 us -> 0.73 us
  matrix products: 12.4 us -> 0 us
    unnamed x3 -> x0, waiting for transfers between devices: 410 us -> none
    pallas_call x0 -> x1, Pallas kernels: none -> 65.7 us  [paired_shards(): pl.pallas_call(gram_kernel, out_shape=(jax.ShapeDtypeStruct((2, width, 12...]
    psum x1 -> x0, blocking collectives: 45.2 us -> none  [shards(): own_ref = lax.psum(local_ref, 'pix')]
    slice x6 -> x0, local copies, waits for them, and re-layouts: 37.5 us -> none  [the longest x1 13.4 us: shards(): raw_terms[:, :, :block_width]]
    all_gather x1 -> x0, waiting for transfers between devices: 16.4 us -> none  [shards(): whole_fields = lax.all_gather(fields, 'mode', axis=2, tiled=True)]
    dot_general x5 -> x0, matrix products: 12.4 us -> none  [the longest x1 4.42 us: shards(): lax.dot_general(own_real, band_real, contract, preferred_element_type=jnp...]
    unnamed x21 -> x4, local copies, waits for them, and re-layouts: 16.3 us -> 4.41 us
    gather x3 -> x0, local copies, waits for them, and re-layouts: 10.3 us -> none  [shards(): jnp.take(tiled, picked, axis=2).reshape(2, pixel_rows, full_width)]
  transfers between devices with their start and end apart: 2 -> 0, of which waited for: 2 -> 0; matrix products, arithmetic and copies ran while one was open for 0% -> 0% of each run, Pallas kernels for 0% -> 0%
where the time goes in v1:
time: 73.6 us; the launch traced here: 72.8 us
  Pallas kernels  65.7 us (89%)
  local copies, waits for them, and re-layouts  4.74 us (6%)
  other arithmetic  1.63 us (2%)
    pallas_call x1, Pallas kernels, paired_shards(): pl.pallas_call(gram_kernel, out_shape=(jax.ShapeDtypeStruct((2, width, 12...  65.7 us
    unnamed x4, local copies, waits for them, and re-layouts  4.41 us

profile of v1, /device:TPU:0, one launch (start us, length us, event | category | flops | bytes accessed | tf_op | source)
XLA Modules:
  0.0 72.8 jit_solution(17181418019703606112)
XLA Ops:
  0.6 0.8 %convert_reduce_fusion = bf16[512]{0:T(512)(128)(2,1)S(1)} fusion(s32[512]{0:T(512)S(1)} %iota_add_fusion, s32[64]{0:T(128)} %param.7), kind=kLoop, calls=%fused_computation.6 | loop fusion | flops 97792 | bytes 3328 | tf_op jit(solution)/shard_map/reduce_sum | solution.py:385
  1.4 0.2 scatter.9.weight_ref
  1.6 0.0 copy-start
  1.7 2.2 %copy-done = bf16[4,512,1024]{2,1,0:T(8,128)(2,1)S(1)} copy-done((bf16[4,512,1024]{2,1,0:T(8,128)(2,1)S(1)}, bf16[4,512,1024]{2,1,0:T(8,128)(2,1)}, u32[]{:S(2)}) %copy-start) | copy-done | bytes 4194328
  3.8 65.7 %shard_map.41 = (f32[2,1024,128]{2,1,0:T(8,128)S(1)}, f32[2,8,1024]{2,1,0:T(8,128)S(1)}) custom-call(bf16[4,512,1024]{2,1,0:T(8,128)(2,1)S(1)} %copy-done, bf16[16,1024]{1,0:T(8,128)(2,1)S(1)} %scatter.9.weight_ref), custom_call_target="tpu_custom_call" | custom-call | tf_op jit(solution)/shard_map/pallas_call | solution.py:397
  69.6 0.1 dynamic-slice.14
  69.7 0.1 dynamic-slice_divide_fusion
  69.8 0.1 pad_maximum_fusion.1
  69.9 0.3 subtract_multiply_fusion
  70.2 0.3 pad_maximum_fusion
  70.6 1.1 %copy.7 = f32[2,1024,64]{1,2,0:T(8,128)} copy(f32[2,1024,64]{2,1,0:T(8,128)S(1)} %get-tuple-element.36) | data formatting | bytes 1048576
  71.7 1.1 %copy.6 = f32[2,1024,64]{1,2,0:T(8,128)} copy(f32[2,1024,64]{2,1,0:T(8,128)S(1)} %get-tuple-element.37) | data formatting | bytes 1048576
  (8 shorter events, 0.1 us)
Async XLA Ops:
  1.6 2.2 %copy-start = (bf16[4,512,1024]{2,1,0:T(8,128)(2,1)S(1)}, bf16[4,512,1024]{2,1,0:T(8,128)(2,1)}, u32[]{:S(2)}) copy-start(bf16[4,512,1024]{2,1,0:T(8,128)(2,1)} %frames_ref.1) | copy-start | bytes 12582916

commit v2 on v1

--- a/solution.py
+++ b/solution.py
@@ -1,3 +1,4 @@
+import functools
 import math
 
 import jax
@@ -90,10 +91,10 @@
 
 
 def gram_kernel(
-    frames_ref, weight_ref, gram_ref, sums_ref,
-    own, other, part, first_in, second_in, outer_in, inner_in, end_in,
+    frames_hbm, pixels_ref, gram_ref, sums_ref,
+    frames_ref, own, other, part, first_in, second_in, outer_in, inner_in, end_in,
     ref_out, ref_in, total, cross_out, cross_in, turn_out, turn_in,
-    field_send, field_recv, first_send, first_recv, second_send, second_recv,
+    frame_sem, field_send, field_recv, first_send, first_recv, second_send, second_recv,
     line_send, outer_recv, inner_recv, end_recv, ref_send, ref_recv,
     cross_send, cross_recv, turn_send, turn_recv,
 ):
@@ -109,12 +110,26 @@
     outer_peer = jnp.where(upper, pix + 4, pix - 4)
     z_even_peer = pix + 4 - 8 * (z % 2)
     z_far_peer = pix + 8 - 16 * (z // 2)
-    pixel_rows = frames_ref.shape[1]
-    width = frames_ref.shape[2]
+    pixel_rows = frames_hbm.shape[1]
+    width = frames_hbm.shape[2]
     rows = NEAR * GROUP
     half = rows // 2
     chunk = 4 * GROUP
 
+    def chunk_z(k):
+        return jnp.where(upper, k, 3 - k)
+
+    def chunk_modes(k):
+        return pl.ds(pl.multiple_of(chunk_z(k) * chunk, chunk), chunk)
+
+    loads = [
+        pltpu.make_async_copy(
+            frames_hbm.at[:, :, chunk_modes(k)], frames_ref.at[k], frame_sem.at[k]
+        )
+        for k in range(4)
+    ]
+    for load in loads:
+        load.start()
     barrier = pltpu.get_barrier_semaphore()
     for step in range(1, 16):
         pl.semaphore_signal(
@@ -129,25 +144,18 @@
         )
         return copy
 
-    def chunk_z(k):
-        return jnp.where(upper, k, 3 - k)
-
-    def field_chunk(k, carry):
-        at = pl.multiple_of(chunk_z(k) * chunk, chunk)
-        cols = pl.ds(at, chunk)
-        real = frames_ref[0, :, cols].astype(jnp.float32) - frames_ref[2, :, cols].astype(jnp.float32)
-        imag = frames_ref[3, :, cols].astype(jnp.float32) - frames_ref[1, :, cols].astype(jnp.float32)
-        own[cols, 0:pixel_rows] = real.astype(jnp.bfloat16).T
-        own[cols, pixel_rows:2 * pixel_rows] = imag.astype(jnp.bfloat16).T
-        return carry
-
-    lax.fori_loop(0, 4, field_chunk, 0)
+    for k in range(4):
+        loads[k].wait()
+        frame = [frames_ref[k, step].astype(jnp.float32) for step in range(4)]
+        modes = chunk_modes(k)
+        own[modes, 0:pixel_rows] = (frame[0] - frame[2]).astype(jnp.bfloat16).T
+        own[modes, pixel_rows:2 * pixel_rows] = (frame[3] - frame[1]).astype(jnp.bfloat16).T
     own[pl.ds(width, 8 * GROUP), :] = own[pl.ds(0, 8 * GROUP), :]
     pl.semaphore_wait(barrier, 16)
 
     def field_copy(k):
-        cols = pl.ds(pl.multiple_of(chunk_z(k) * chunk, chunk), chunk)
-        return send(own.at[cols], other.at[cols], field_send.at[k], field_recv.at[k], pix, 1 - mode)
+        modes = chunk_modes(k)
+        return send(own.at[modes], other.at[modes], field_send.at[k], field_recv.at[k], pix, 1 - mode)
 
     field_copies = [field_copy(k) for k in range(4)]
     for copy in field_copies:
@@ -288,8 +296,19 @@
 
     begin(0)
     begin(1)
+    positions = pix * pixel_rows + lax.broadcasted_iota(
+        jnp.int32, (pixels_ref.shape[0], pixel_rows), 1
+    )
+    counts = jnp.sum(
+        jnp.where(pixels_ref[...] == positions, 1.0, 0.0), axis=0, keepdims=True
+    )
+    nothing = jnp.zeros_like(counts)
+    row = lax.broadcasted_iota(jnp.int32, (16, 2 * pixel_rows), 0)
+    real_weight = jnp.concatenate([counts, nothing], axis=1)
+    imag_weight = jnp.concatenate([nothing, counts], axis=1)
+    weight = jnp.where(row == 0, real_weight, jnp.where(row == 1, imag_weight, 0.0))
     ref_out[0] = lax.dot_general(
-        weight_ref[...], own[pl.ds(0, width), :], contract, preferred_element_type=jnp.float32
+        weight.astype(jnp.bfloat16), own[pl.ds(0, width), :], contract, preferred_element_type=jnp.float32
     )[0:8]
     ref_copies[0].start()
     forward(0)
@@ -377,19 +396,38 @@
         line_copy(3, "end").wait_send()
 
 
+def finish_kernel(pixel_scale, gram_ref, sums_ref, band_ref, diag_ref):
+    pix = lax.axis_index("pix")
+    odd = pix % 2 == 1
+    at = pl.multiple_of((pix // 2) * 128, 128)
+    own = sums_ref[0, :, pl.ds(at, 128)]
+    other = sums_ref[1, :, pl.ds(at, 128)]
+    low = lax.broadcasted_iota(jnp.int32, own.shape, 1) < GROUP
+    own = jnp.where(odd, pltpu.roll(own, GROUP, 1), own)
+    other = jnp.where(odd, other, pltpu.roll(other, GROUP, 1))
+    cols = jnp.where(low, own, other).T
+
+    def unit(real, imag):
+        magnitude = jnp.maximum(jnp.sqrt(real * real + imag * imag), 1.0)
+        return real / magnitude, imag / magnitude
+
+    col_real, col_imag = unit(cols[:, 0:1], cols[:, 1:2])
+    row_real, row_imag = unit(sums_ref[0, 0:1, :], sums_ref[0, 1:2, :])
+    unit_real = row_real * col_real + row_imag * col_imag
+    unit_imag = row_imag * col_real - row_real * col_imag
+    gram_real = gram_ref[0].T
+    gram_imag = gram_ref[1].T
+    real = (unit_real * gram_real - unit_imag * gram_imag) * pixel_scale
+    imag = (unit_real * gram_imag + unit_imag * gram_real) * pixel_scale
+    diag_ref[0] = real[:GROUP]
+    diag_ref[1] = imag[:GROUP]
+    band_ref[0] = real[GROUP:]
+    band_ref[1] = imag[GROUP:]
+
+
 def paired_shards(frames, ref_pixels):
-    pix_index = lax.axis_index("pix")
     pixel_rows = frames.shape[1]
     width = frames.shape[2]
-    positions = pix_index * pixel_rows + lax.iota(jnp.int32, pixel_rows)
-    counts = jnp.sum(
-        (ref_pixels[:, None] == positions[None, :]).astype(jnp.float32), axis=0
-    ).astype(jnp.bfloat16)
-    weight = (
-        jnp.zeros((16, 2 * pixel_rows), jnp.bfloat16)
-        .at[0, :pixel_rows].set(counts)
-        .at[1, pixel_rows:].set(counts)
-    )
     rows = NEAR * GROUP
     half = rows // 2
     b16 = jnp.bfloat16
@@ -400,9 +438,13 @@
             jax.ShapeDtypeStruct((2, width, 128), jnp.float32),
             jax.ShapeDtypeStruct((2, 8, width), jnp.float32),
         ),
-        in_specs=[pl.BlockSpec(memory_space=pltpu.VMEM)] * 2,
+        in_specs=[
+            pl.BlockSpec(memory_space=pltpu.HBM),
+            pl.BlockSpec(memory_space=pltpu.VMEM),
+        ],
         out_specs=(pl.BlockSpec(memory_space=pltpu.VMEM),) * 2,
         scratch_shapes=[
+            pltpu.VMEM((4, 4, pixel_rows, 4 * GROUP), b16),
             pltpu.VMEM((width + 8 * GROUP, 2 * pixel_rows), b16),
             pltpu.VMEM((width, 2 * pixel_rows), b16),
             pltpu.VMEM((16, rows, 256), b16),
@@ -418,7 +460,7 @@
             pltpu.VMEM((FAR * GROUP, 128), b16),
             pltpu.VMEM((FAR, 128, 128), b16),
             pltpu.VMEM((FAR, 128, 128), b16),
-            dma((4,)), dma((4,)),
+            dma((4,)), dma((4,)), dma((4,)),
             dma((2, 4, 2)), dma((2, 4, 2)),
             dma((2, 4)), dma((2, 4)),
             dma((4,)), dma((3,)), dma((2,)), dma,
@@ -427,22 +469,17 @@
             dma((FAR,)), dma((FAR,)),
         ],
         compiler_params=pltpu.CompilerParams(
-            collective_id=0, has_side_effects=True, vmem_limit_bytes=48 * 1024 * 1024
+            collective_id=0, has_side_effects=True, vmem_limit_bytes=61 * 1024 * 1024
         ),
-    )(frames, weight)
-    phase_own = unit_phase(sums[0, :2])
-    phase_other = unit_phase(sums[1, :2])
-    start = pix_index * GROUP
-    cols = jnp.concatenate(
-        [
-            lax.dynamic_slice_in_dim(phase_own, start, GROUP, 1),
-            lax.dynamic_slice_in_dim(phase_other, start, GROUP, 1),
-        ],
-        axis=1,
-    )
+    )(frames, ref_pixels.reshape(-1, 1))
     pixel_scale = 1.0 / math.sqrt(lax.axis_size("pix") * pixel_rows)
-    turned = rotate(gram[0], gram[1], phase_own, cols, pixel_scale)
-    return (turned[:, :, GROUP:], turned[:, :, :GROUP])
+    band, diag = pl.pallas_call(
+        functools.partial(finish_kernel, pixel_scale),
+        out_shape=(jax.ShapeDtypeStruct((2, GROUP, width), jnp.float32),) * 2,
+        in_specs=[pl.BlockSpec(memory_space=pltpu.VMEM)] * 2,
+        out_specs=(pl.BlockSpec(memory_space=pltpu.VMEM),) * 2,
+    )(gram, sums)
+    return (jnp.swapaxes(band, 1, 2), jnp.swapaxes(diag, 1, 2))
 
 
 def solution(mesh):

time: 73.6 us -> 73.1 us (level)
  Pallas kernels: 65.7 us -> 70 us
  local copies, waits for them, and re-layouts: 4.74 us -> 1.36 us
  other arithmetic: 1.63 us -> 0 us
    unnamed x4 -> x0, local copies, waits for them, and re-layouts: 4.41 us -> none
    pallas_call x0 -> x1, Pallas kernels: none -> 2.86 us  [paired_shards(): pl.pallas_call(functools.partial(finish_kernel, pixel_scale), out_shape=(...]
    pallas_call x1, Pallas kernels: 65.7 us -> 67.1 us  [paired_shards(): pl.pallas_call(gram_kernel, out_shape=(jax.ShapeDtypeStruct((2, width, 12...]
    reshape x0 -> x1, local copies, waits for them, and re-layouts: none -> 1.36 us  [paired_shards(): ref_pixels.reshape(-1, 1)]
    reduce_sum x1 -> x0, other arithmetic: 0.75 us -> none  [paired_shards(): jnp.sum((ref_pixels[:, None] == positions[None, :]).astype(jnp.float32),...]
where the time goes in v2:
time: 73.1 us; the launch traced here: 72 us
  Pallas kernels  70 us (96%)
  local copies, waits for them, and re-layouts  1.36 us (2%)
    pallas_call x1, Pallas kernels, paired_shards(): pl.pallas_call(gram_kernel, out_shape=(jax.ShapeDtypeStruct((2, width, 12...  67.1 us
    pallas_call x1, Pallas kernels, paired_shards(): pl.pallas_call(functools.partial(finish_kernel, pixel_scale), out_shape=(...  2.86 us

profile of v2, /device:TPU:0, one launch (start us, length us, event | category | flops | bytes accessed | tf_op | source)
XLA Modules:
  0.0 72.0 jit_solution(11632575505609864754)
XLA Ops:
  0.6 1.4 %copy.4.pixels_ref = s32[64,1]{1,0:T(8,128)} copy(s32[64,1]{0,1:T(1,128)} %bitcast.3) | data formatting | bytes 512 | tf_op jit(solution)/shard_map/reshape | solution.py:474
  2.0 67.1 %shard_map.41 = (f32[2,1024,128]{2,1,0:T(8,128)}, f32[2,8,1024]{2,1,0:T(8,128)}) custom-call(bf16[4,512,1024]{2,1,0:T(8,128)(2,1)} %frames_hbm.1, s32[64,1]{1,0:T(8,128)} %copy.4.pixels_ref), custom_call_target="tpu_custom_call" | custom-call | tf_op jit(solution)/shard_map/pallas_call | solution.py:435
  69.1 2.9 %shard_map.42 = (f32[2,64,1024]{2,1,0:T(8,128)}, f32[2,64,1024]{2,1,0:T(8,128)}) custom-call(f32[2,1024,128]{2,1,0:T(8,128)} %get-tuple-element.6.gram_ref, f32[2,8,1024]{2,1,0:T(8,128)} %get-tuple-element.7.sums_ref), custom_call_target="tpu_custom_call" | custom-call | tf_op jit(solution)/shard_map/pallas_call | solution.py:476

commit v3 on v2

--- a/solution.py
+++ b/solution.py
@@ -87,15 +87,20 @@
 MESH = pl.DeviceIdType.MESH
 GROUP = 64
 NEAR = 9
+SIDE = 224
+LAST = 128
 FAR = 7
 
 
 def gram_kernel(
     frames_hbm, pixels_ref, gram_ref, sums_ref,
     frames_ref, own, other, part, first_in, second_in, outer_in, inner_in, end_in,
+    last_outer_in, last_inner_in, last_end_in, last_first_in, last_second_in,
     ref_out, ref_in, total, cross_out, cross_in, turn_out, turn_in,
     frame_sem, field_send, field_recv, first_send, first_recv, second_send, second_recv,
-    line_send, outer_recv, inner_recv, end_recv, ref_send, ref_recv,
+    line_send, outer_recv, inner_recv, end_recv,
+    last_send, last_outer_recv, last_inner_recv, last_end_recv,
+    last_first_send, last_first_recv, last_second_send, last_second_recv, ref_send, ref_recv,
     cross_send, cross_recv, turn_send, turn_recv,
 ):
     pix = lax.axis_index("pix")
@@ -113,7 +118,6 @@
     pixel_rows = frames_hbm.shape[1]
     width = frames_hbm.shape[2]
     rows = NEAR * GROUP
-    half = rows // 2
     chunk = 4 * GROUP
 
     def chunk_z(k):
@@ -202,7 +206,10 @@
 
         lax.fori_loop(0, 4, one, 0)
 
-    spans = [pl.ds(0, half), pl.ds(half, half)]
+    spans = [pl.ds(0, SIDE), pl.ds(SIDE, SIDE)]
+    both = pl.ds(0, 2 * SIDE)
+    last = pl.ds(2 * SIDE, LAST)
+    last_spans = [pl.ds(2 * SIDE, LAST // 2), pl.ds(2 * SIDE + LAST // 2, LAST // 2)]
 
     def owner_of(k, yy, xx):
         return chunk_z(k) * 4 + yy * 2 + xx
@@ -234,8 +241,7 @@
     def f32(value):
         return value.astype(jnp.float32)
 
-    def begin(k):
-        multiply(k)
+    def start_first(k):
         for j in range(2):
             for a in range(2):
                 firsts[a, k, j].start()
@@ -258,7 +264,7 @@
         else:
             dst, sem = end_in, end_recv
         return send(
-            part.at[owner], dst, line_send.at[k], sem,
+            part.at[owner, both], dst, line_send.at[k], sem,
             outer_peer if to == "end" else inner_peer, mode,
         )
 
@@ -291,16 +297,115 @@
             else:
                 line_copy(0, "inner").wait_recv()
                 arrived = inner_in[0]
-            part[owner] = (f32(part[owner]) + f32(arrived)).astype(jnp.bfloat16)
+            part[owner, both] = (f32(part[owner, both]) + f32(arrived)).astype(jnp.bfloat16)
             line_copy(k, "inner" if k < 2 else "end").start()
 
-    begin(0)
-    begin(1)
+    def last_copy(k, to):
+        owners = pl.ds(chunk_z(k) * 4, 4)
+        if to == "outer":
+            dst, sem = last_outer_in.at[k], last_outer_recv.at[k]
+        elif to == "inner":
+            dst, sem = last_inner_in.at[k], last_inner_recv.at[k]
+        else:
+            dst, sem = last_end_in, last_end_recv
+        return send(
+            part.at[owners, last], dst, last_send.at[k], sem,
+            outer_peer if to == "end" else inner_peer, mode,
+        )
+
+    def last_begin(k):
+        @pl.when(is_end)
+        def _():
+            last_copy(k, "outer").start()
+
+    def last_add(k, terms):
+        first = chunk_z(k) * 4
+        for i in range(4):
+            value = f32(part[first + i, last])
+            for term in terms:
+                value = value + f32(term[i])
+            part[first + i, last] = value.astype(jnp.bfloat16)
+
+    def last_pass(k):
+        @pl.when(is_mid)
+        def _():
+            if k < 2:
+                last_copy(k, "outer").wait_recv()
+                last_add(k, [last_outer_in.at[k]])
+                last_copy(k, "inner").start()
+            else:
+                last_copy(0, "inner").wait_recv()
+                last_add(k, [last_inner_in.at[0]])
+                last_copy(k, "end").start()
+
+    def last_first_copy(axis, j):
+        if axis == 0:
+            owner = z * 4 + (1 - y if j == 0 else y) * 2 + 1 - x
+        else:
+            owner = z * 4 + (1 - y) * 2 + (1 - x if j == 0 else x)
+        return send(
+            part.at[owner, last_spans[axis]], last_first_in.at[axis, j],
+            last_first_send.at[axis, j], last_first_recv.at[axis, j],
+            x_peer if axis == 0 else y_peer, mode,
+        )
+
+    def last_second_owner(axis):
+        return z * 4 + (1 - y) * 2 + x if axis == 0 else z * 4 + y * 2 + 1 - x
+
+    def last_second_copy(axis):
+        return send(
+            part.at[last_second_owner(axis), last_spans[axis]], last_second_in.at[axis],
+            last_second_send.at[axis], last_second_recv.at[axis],
+            y_peer if axis == 0 else x_peer, mode,
+        )
+
+    last_firsts = {(a, j): last_first_copy(a, j) for a in range(2) for j in range(2)}
+    last_seconds = [last_second_copy(a) for a in range(2)]
+
+    def last_spread():
+        @pl.when(is_mid)
+        def _():
+            last_copy(2, "outer").wait_recv()
+            last_copy(1, "inner").wait_recv()
+            last_add(2, [last_outer_in.at[2], last_inner_in.at[1]])
+
+        @pl.when(is_end)
+        def _():
+            last_copy(3, "end").wait_recv()
+            last_add(3, [last_end_in])
+
+        for j in range(2):
+            for a in range(2):
+                last_firsts[a, j].start()
+
+    def last_forward():
+        for a in range(2):
+            last_firsts[a, 0].wait_recv()
+            owner = last_second_owner(a)
+            part[owner, last_spans[a]] = (
+                f32(part[owner, last_spans[a]]) + f32(last_first_in[a, 0])
+            ).astype(jnp.bfloat16)
+            last_seconds[a].start()
+
+    def last_keep():
+        for a in range(2):
+            last_firsts[a, 1].wait_recv()
+            last_seconds[a].wait_recv()
+            total[last_spans[a], :] = (
+                f32(part[pix, last_spans[a]]) + f32(last_first_in[a, 1]) + f32(last_second_in[a])
+            )
+
+    for k in range(3):
+        multiply(k)
+        if k < 2:
+            start_first(k)
+        last_begin(k)
     positions = pix * pixel_rows + lax.broadcasted_iota(
-        jnp.int32, (pixels_ref.shape[0], pixel_rows), 1
+        jnp.int32, (pixels_ref.shape[1], pixel_rows), 1
     )
+    listed = jnp.broadcast_to(pixels_ref[...], (8, pixels_ref.shape[1])).T[:, 0:1]
     counts = jnp.sum(
-        jnp.where(pixels_ref[...] == positions, 1.0, 0.0), axis=0, keepdims=True
+        jnp.where(listed == positions, 1.0, 0.0), axis=0, keepdims=True
     )
     nothing = jnp.zeros_like(counts)
     row = lax.broadcasted_iota(jnp.int32, (16, 2 * pixel_rows), 0)
@@ -312,20 +417,27 @@
     )[0:8]
     ref_copies[0].start()
     forward(0)
-    begin(2)
+    start_first(2)
+    multiply(3)
     ref_next(0)
+    last_pass(0)
     forward(1)
+    start_first(3)
+    last_pass(1)
+    ref_next(1)
     keep(0)
-    begin(3)
-    ref_next(1)
     forward(2)
+    last_pass(3)
+    ref_next(2)
+    last_spread()
     keep(1)
     pass_on(0)
-    ref_next(2)
+    ref_next(3)
     forward(3)
+    last_forward()
     keep(2)
     pass_on(1)
-    ref_next(3)
+    last_keep()
     keep(3)
     pass_on(3)
 
@@ -333,12 +445,12 @@
     def _():
         line_copy(2, "outer").wait_recv()
         line_copy(1, "inner").wait_recv()
-        total[...] = total[...] + f32(outer_in[2]) + f32(inner_in[1])
+        total[both, :] = total[both, :] + f32(outer_in[2]) + f32(inner_in[1])
 
     @pl.when(is_end)
     def _():
         line_copy(3, "end").wait_recv()
-        total[...] = total[...] + f32(end_in[...])
+        total[both, :] = total[both, :] + f32(end_in[...])
 
     cross_out[...] = total[GROUP:8 * GROUP, 128:256].astype(jnp.bfloat16)
     cross = send(cross_out, cross_in, cross_send, cross_recv, pix, 1 - mode)
@@ -384,16 +496,18 @@
 
     for copy in field_copies + ref_copies + list(firsts.values()) + list(seconds.values()):
         copy.wait_send()
-    for copy in turns + [cross]:
+    for copy in turns + [cross] + list(last_firsts.values()) + last_seconds:
         copy.wait_send()
     for k in range(3):
         @pl.when(is_end | (k < 2))
         def _():
             line_copy(k, "outer").wait_send()
+            last_copy(k, "outer").wait_send()
 
     @pl.when(is_mid)
     def _():
         line_copy(3, "end").wait_send()
+        last_copy(3, "end").wait_send()
 
 
 def finish_kernel(pixel_scale, gram_ref, sums_ref, band_ref, diag_ref):
@@ -429,7 +543,6 @@
     pixel_rows = frames.shape[1]
     width = frames.shape[2]
     rows = NEAR * GROUP
-    half = rows // 2
     b16 = jnp.bfloat16
     dma = pltpu.SemaphoreType.DMA
     gram, sums = pl.pallas_call(
@@ -448,11 +561,16 @@
             pltpu.VMEM((width + 8 * GROUP, 2 * pixel_rows), b16),
             pltpu.VMEM((width, 2 * pixel_rows), b16),
             pltpu.VMEM((16, rows, 256), b16),
-            pltpu.VMEM((2, 4, 2, half, 256), b16),
-            pltpu.VMEM((2, 4, half, 256), b16),
-            pltpu.VMEM((3, rows, 256), b16),
-            pltpu.VMEM((2, rows, 256), b16),
-            pltpu.VMEM((rows, 256), b16),
+            pltpu.VMEM((2, 4, 2, SIDE, 256), b16),
+            pltpu.VMEM((2, 4, SIDE, 256), b16),
+            pltpu.VMEM((3, 2 * SIDE, 256), b16),
+            pltpu.VMEM((2, 2 * SIDE, 256), b16),
+            pltpu.VMEM((2 * SIDE, 256), b16),
+            pltpu.VMEM((3, 4, LAST, 256), b16),
+            pltpu.VMEM((2, 4, LAST, 256), b16),
+            pltpu.VMEM((4, LAST, 256), b16),
+            pltpu.VMEM((2, 2, LAST // 2, 256), b16),
+            pltpu.VMEM((2, LAST // 2, 256), b16),
             pltpu.VMEM((5, 8, width), jnp.float32),
             pltpu.VMEM((5, 8, width), jnp.float32),
             pltpu.VMEM((rows, 256), jnp.float32),
@@ -464,14 +582,16 @@
             dma((2, 4, 2)), dma((2, 4, 2)),
             dma((2, 4)), dma((2, 4)),
             dma((4,)), dma((3,)), dma((2,)), dma,
+            dma((4,)), dma((3,)), dma((2,)), dma,
+            dma((2, 2)), dma((2, 2)), dma((2,)), dma((2,)),
             dma((5,)), dma((5,)),
             dma, dma,
             dma((FAR,)), dma((FAR,)),
         ],
         compiler_params=pltpu.CompilerParams(
-            collective_id=0, has_side_effects=True, vmem_limit_bytes=61 * 1024 * 1024
+            collective_id=0, has_side_effects=True, vmem_limit_bytes=55 * 1024 * 1024
         ),
-    )(frames, ref_pixels.reshape(-1, 1))
+    )(frames, ref_pixels.reshape(1, -1))
     pixel_scale = 1.0 / math.sqrt(lax.axis_size("pix") * pixel_rows)
     band, diag = pl.pallas_call(
         functools.partial(finish_kernel, pixel_scale),

time: 73.1 us -> 68.3 us (0.934); the launches traced: 72 us -> 68.1 us
  Pallas kernels: 70 us -> 67.5 us
  local copies, waits for them, and re-layouts: 1.36 us -> 0 us
    pallas_call x1, Pallas kernels: 67.1 us -> 64.7 us  [paired_shards(): pl.pallas_call(gram_kernel, out_shape=(jax.ShapeDtypeStruct((2, width, 12...]
    reshape x1 -> x0, local copies, waits for them, and re-layouts: 1.36 us -> none  [paired_shards(): ref_pixels.reshape(-1, 1)]
where the time goes in v3:
time: 68.3 us; the launch traced here: 68.1 us
  Pallas kernels  67.5 us (99%)
    pallas_call x1, Pallas kernels, paired_shards(): pl.pallas_call(gram_kernel, out_shape=(jax.ShapeDtypeStruct((2, width, 12...  64.7 us
    pallas_call x1, Pallas kernels, paired_shards(): pl.pallas_call(functools.partial(finish_kernel, pixel_scale), out_shape=(...  2.86 us

profile of v3, /device:TPU:0, one launch (start us, length us, event | category | flops | bytes accessed | tf_op | source)
XLA Modules:
  0.0 68.1 jit_solution(2407093118490701437)
XLA Ops:
  0.6 64.7 %shard_map.41 = (f32[2,1024,128]{2,1,0:T(8,128)}, f32[2,8,1024]{2,1,0:T(8,128)}) custom-call(bf16[4,512,1024]{2,1,0:T(8,128)(2,1)} %frames_hbm.1, s32[1,64]{1,0:T(1,128)} %bitcast.3), custom_call_target="tpu_custom_call" | custom-call | tf_op jit(solution)/shard_map/pallas_call | solution.py:548
  65.3 2.9 %shard_map.42 = (f32[2,64,1024]{2,1,0:T(8,128)}, f32[2,64,1024]{2,1,0:T(8,128)}) custom-call(f32[2,1024,128]{2,1,0:T(8,128)} %get-tuple-element.6.gram_ref, f32[2,8,1024]{2,1,0:T(8,128)} %get-tuple-element.7.sums_ref), custom_call_target="tpu_custom_call" | custom-call | tf_op jit(solution)/shard_map/pallas_call | solution.py:596

commit v4 on v3

--- a/solution.py
+++ b/solution.py
@@ -148,20 +148,28 @@
         )
         return copy
 
+    def ring_rows(zz, column):
+        return pl.ds(pl.multiple_of((column * 4 + zz) * GROUP, GROUP), GROUP)
+
     for k in range(4):
         loads[k].wait()
         frame = [frames_ref[k, step].astype(jnp.float32) for step in range(4)]
-        modes = chunk_modes(k)
-        own[modes, 0:pixel_rows] = (frame[0] - frame[2]).astype(jnp.bfloat16).T
-        own[modes, pixel_rows:2 * pixel_rows] = (frame[3] - frame[1]).astype(jnp.bfloat16).T
+        real = (frame[0] - frame[2]).astype(jnp.bfloat16).T
+        imag = (frame[3] - frame[1]).astype(jnp.bfloat16).T
+        for i in range(4):
+            to = ring_rows(chunk_z(k), i)
+            own[to, 0:pixel_rows] = real[i * GROUP:(i + 1) * GROUP]
+            own[to, pixel_rows:2 * pixel_rows] = imag[i * GROUP:(i + 1) * GROUP]
     own[pl.ds(width, 8 * GROUP), :] = own[pl.ds(0, 8 * GROUP), :]
     pl.semaphore_wait(barrier, 16)
 
-    def field_copy(k):
-        modes = chunk_modes(k)
-        return send(own.at[modes], other.at[modes], field_send.at[k], field_recv.at[k], pix, 1 - mode)
-
-    field_copies = [field_copy(k) for k in range(4)]
+    def field_copy(k, i):
+        at = ring_rows(chunk_z(k), i)
+        return send(
+            own.at[at], other.at[at], field_send.at[k, i], field_recv.at[k, i], pix, 1 - mode
+        )
+
+    field_copies = [field_copy(k, i) for k in range(4) for i in range(4)]
     for copy in field_copies:
         copy.start()
 
@@ -187,24 +195,22 @@
 
     def multiply(k):
         zc = chunk_z(k)
-        field_copies[k].wait_recv()
-
-        def one(t, carry):
-            yy = jnp.where(t % 2 == 0, 1 - y, y)
-            xx = jnp.where(t < 2, 1 - x, x)
-            owner = zc * 4 + yy * 2 + xx
-            at = pl.multiple_of(owner * GROUP, GROUP)
-            own_cols = own[pl.ds(at, GROUP), :]
-            other_cols = other[pl.ds(at, GROUP), :]
+        for i in range(4):
+            field_copies[4 * k + i].wait_recv()
+        for t in range(4):
+            column = (1 - y if t % 2 == 0 else y) * 2 + (1 - x if t < 2 else x)
+            start = pl.multiple_of((column * 4 + zc) * GROUP, GROUP)
+            own_cols = own[pl.ds(start, GROUP), :]
+            other_cols = other[pl.ds(start, GROUP), :]
             cols = jnp.concatenate(
                 [own_cols, turned(own_cols), other_cols, turned(other_cols)], axis=0
             )
-            left = own[pl.ds(at, rows), :]
+            left = own[pl.ds(start, rows), :]
             out = lax.dot_general(left, cols, contract, preferred_element_type=jnp.float32)
-            part[owner] = out.astype(jnp.bfloat16)
-            return carry
-
-        lax.fori_loop(0, 4, one, 0)
+            part[zc * 4 + column] = out.astype(jnp.bfloat16)
+            if k < 2:
+                for a, j in (((0, 0), (1, 0)), ((0, 1),), ((1, 1),), ())[t]:
+                    firsts[a, k, j].start()
 
     spans = [pl.ds(0, SIDE), pl.ds(SIDE, SIDE)]
     both = pl.ds(0, 2 * SIDE)
@@ -395,10 +401,43 @@
                 f32(part[pix, last_spans[a]]) + f32(last_first_in[a, 1]) + f32(last_second_in[a])
             )
 
+    rest = (FAR - 1) * GROUP
+    ring = pix % 4 * 4 + z
+
+    def chip_at(step):
+        there = (ring + step) % 16
+        return there % 4 * 4 + there // 4
+
+    def cross_copy(at, size, index):
+        rows_at = pl.ds(at, size)
+        return send(
+            cross_out.at[rows_at], cross_in.at[rows_at],
+            cross_send.at[index], cross_recv.at[index], pix, 1 - mode,
+        )
+
+    cross_rest = cross_copy(0, rest, 0)
+    cross_early = cross_copy(rest, GROUP, 1)
+    turns = [
+        send(
+            turn_out.at[d - 1], turn_in.at[d - 1], turn_send.at[d - 1], turn_recv.at[d - 1],
+            chip_at(d), mode,
+        )
+        for d in range(1, FAR + 1)
+    ]
+
+    def start_turn(d):
+        stacked = jnp.concatenate(
+            [
+                total[d * GROUP:(d + 1) * GROUP, 0:128].astype(jnp.bfloat16),
+                cross_in[(d - 1) * GROUP:d * GROUP, :],
+            ],
+            axis=0,
+        )
+        turn_out[d - 1] = stacked.T
+        turns[d - 1].start()
+
     for k in range(3):
         multiply(k)
-        if k < 2:
-            start_first(k)
         last_begin(k)
     positions = pix * pixel_rows + lax.broadcasted_iota(
         jnp.int32, (pixels_ref.shape[1], pixel_rows), 1
@@ -412,9 +451,13 @@
     real_weight = jnp.concatenate([counts, nothing], axis=1)
     imag_weight = jnp.concatenate([nothing, counts], axis=1)
     weight = jnp.where(row == 0, real_weight, jnp.where(row == 1, imag_weight, 0.0))
-    ref_out[0] = lax.dot_general(
-        weight.astype(jnp.bfloat16), own[pl.ds(0, width), :], contract, preferred_element_type=jnp.float32
-    )[0:8]
+    weight = weight.astype(jnp.bfloat16)
+    for pair in range(8):
+        places = [(p % 4 * 4 + p // 4) * GROUP for p in (2 * pair, 2 * pair + 1)]
+        block = jnp.concatenate([own[pl.ds(at, GROUP), :] for at in places], axis=0)
+        ref_out[0, :, pl.ds(pair * 128, 128)] = lax.dot_general(
+            weight, block, contract, preferred_element_type=jnp.float32
+        )[0:8]
     ref_copies[0].start()
     forward(0)
     start_first(2)
@@ -438,8 +481,13 @@
     keep(2)
     pass_on(1)
     last_keep()
+    cross_out[rest:] = total[FAR * GROUP:NEAR * GROUP - GROUP, 128:256].astype(jnp.bfloat16)
+    cross_early.start()
     keep(3)
     pass_on(3)
+
+    cross_early.wait_recv()
+    start_turn(FAR)
 
     @pl.when(is_mid)
     def _():
@@ -452,15 +500,14 @@
         line_copy(3, "end").wait_recv()
         total[both, :] = total[both, :] + f32(end_in[...])
 
-    cross_out[...] = total[GROUP:8 * GROUP, 128:256].astype(jnp.bfloat16)
-    cross = send(cross_out, cross_in, cross_send, cross_recv, pix, 1 - mode)
-    cross.start()
+    cross_out[0:rest] = total[GROUP:FAR * GROUP, 128:256].astype(jnp.bfloat16)
+    cross_rest.start()
 
     lane = lax.broadcasted_iota(jnp.int32, (GROUP, 128), 1)
     low = lane < GROUP
 
     def group_rows(step):
-        return pl.ds(pl.multiple_of(((pix + step) % 16) * GROUP, GROUP), GROUP)
+        return pl.ds(pl.multiple_of(chip_at(step) * GROUP, GROUP), GROUP)
 
     for d in range(NEAR):
         here = total[d * GROUP:(d + 1) * GROUP, 0:128]
@@ -468,23 +515,9 @@
         gram_ref[0, group_rows(d), :] = jnp.where(low, here, pltpu.roll(there, GROUP, 1))
         gram_ref[1, group_rows(d), :] = jnp.where(low, pltpu.roll(here, GROUP, 1), there)
 
-    cross.wait_recv()
-    turns = []
-    for d in range(1, FAR + 1):
-        stacked = jnp.concatenate(
-            [
-                total[d * GROUP:(d + 1) * GROUP, 0:128].astype(jnp.bfloat16),
-                cross_in[(d - 1) * GROUP:d * GROUP, :],
-            ],
-            axis=0,
-        )
-        turn_out[d - 1] = stacked.T
-        turn = send(
-            turn_out.at[d - 1], turn_in.at[d - 1], turn_send.at[d - 1], turn_recv.at[d - 1],
-            (pix + d) % 16, mode,
-        )
-        turn.start()
-        turns.append(turn)
+    cross_rest.wait_recv()
+    for d in range(1, FAR):
+        start_turn(d)
     ref_copies[4].wait_recv()
     sums_ref[0] = ref_out[4]
     sums_ref[1] = ref_in[4]
@@ -496,7 +529,7 @@
 
     for copy in field_copies + ref_copies + list(firsts.values()) + list(seconds.values()):
         copy.wait_send()
-    for copy in turns + [cross] + list(last_firsts.values()) + last_seconds:
+    for copy in turns + [cross_rest, cross_early] + list(last_firsts.values()) + last_seconds:
         copy.wait_send()
     for k in range(3):
         @pl.when(is_end | (k < 2))
@@ -578,18 +611,18 @@
             pltpu.VMEM((FAR * GROUP, 128), b16),
             pltpu.VMEM((FAR, 128, 128), b16),
             pltpu.VMEM((FAR, 128, 128), b16),
-            dma((4,)), dma((4,)), dma((4,)),
+            dma((4,)), dma((4, 4)), dma((4, 4)),
             dma((2, 4, 2)), dma((2, 4, 2)),
             dma((2, 4)), dma((2, 4)),
             dma((4,)), dma((3,)), dma((2,)), dma,
             dma((4,)), dma((3,)), dma((2,)), dma,
             dma((2, 2)), dma((2, 2)), dma((2,)), dma((2,)),
             dma((5,)), dma((5,)),
-            dma, dma,
+            dma((2,)), dma((2,)),
             dma((FAR,)), dma((FAR,)),
         ],
         compiler_params=pltpu.CompilerParams(
-            collective_id=0, has_side_effects=True, vmem_limit_bytes=55 * 1024 * 1024
+            collective_id=0, has_side_effects=True, vmem_limit_bytes=52 * 1024 * 1024
         ),
     )(frames, ref_pixels.reshape(1, -1))
     pixel_scale = 1.0 / math.sqrt(lax.axis_size("pix") * pixel_rows)

time: 68.3 us -> 67.2 us (0.984)
  Pallas kernels: 67.5 us -> 64.1 us
  local copies, waits for them, and re-layouts: 0 us -> 2.23 us
    pallas_call x1, Pallas kernels: 64.7 us -> 61.2 us  [paired_shards(): pl.pallas_call(gram_kernel, out_shape=(jax.ShapeDtypeStruct((2, width, 12...]
    unnamed x0 -> x6, local copies, waits for them, and re-layouts: none -> 2.23 us
where the time goes in v4:
time: 67.2 us; the launch traced here: 67 us
  Pallas kernels  64.1 us (95%)
  local copies, waits for them, and re-layouts  2.23 us (3%)
    pallas_call x1, Pallas kernels, paired_shards(): pl.pallas_call(gram_kernel, out_shape=(jax.ShapeDtypeStruct((2, width, 12...  61.2 us
    pallas_call x1, Pallas kernels, paired_shards(): pl.pallas_call(functools.partial(finish_kernel, pixel_scale), out_shape=(...  2.86 us
    unnamed x6, local copies, waits for them, and re-layouts  2.23 us

profile of v4, /device:TPU:0, one launch (start us, length us, event | category | flops | bytes accessed | tf_op | source)
XLA Modules:
  0.0 67.0 jit_solution(15681985539539494454)
XLA Ops:
  0.6 0.0 copy-start.2
  0.6 0.6 copy-done.2
  1.3 61.2 %shard_map.41 = (f32[2,1024,128]{2,1,0:T(8,128)S(1)}, f32[2,8,1024]{2,1,0:T(8,128)S(1)}) custom-call(bf16[4,512,1024]{2,1,0:T(8,128)(2,1)} %frames_hbm.1, s32[1,64]{1,0:T(1,128)S(1)} %bitcast.3), custom_call_target="tpu_custom_call" | custom-call | tf_op jit(solution)/shard_map/pallas_call | solution.py:581
  62.5 0.0 copy-start
  62.5 1.0 %copy-done = f32[2,1024,128]{2,1,0:T(8,128)} copy-done((f32[2,1024,128]{2,1,0:T(8,128)}, f32[2,1024,128]{2,1,0:T(8,128)S(1)}, u32[]{:S(2)}) %copy-start) | copy-done | bytes 1048600
  63.5 0.0 copy-start.1
  63.5 0.6 copy-done.1
  64.1 2.9 %shard_map.42 = (f32[2,64,1024]{2,1,0:T(8,128)}, f32[2,64,1024]{2,1,0:T(8,128)}) custom-call(f32[2,1024,128]{2,1,0:T(8,128)} %copy-done, f32[2,8,1024]{2,1,0:T(8,128)} %copy-done.1), custom_call_target="tpu_custom_call" | custom-call | tf_op jit(solution)/shard_map/pallas_call | solution.py:629
Async XLA Ops:
  0.6 0.7 copy-start.2
  62.5 1.0 %copy-start = (f32[2,1024,128]{2,1,0:T(8,128)}, f32[2,1024,128]{2,1,0:T(8,128)S(1)}, u32[]{:S(2)}) copy-start(f32[2,1024,128]{2,1,0:T(8,128)S(1)} %get-tuple-element.6.gram_ref) | copy-start | bytes 3145732
  63.5 0.6 copy-start.1

commit v5 on v4

--- a/solution.py
+++ b/solution.py
@@ -88,6 +88,7 @@
 GROUP = 64
 NEAR = 9
 SIDE = 224
+EARLY = 3
 LAST = 128
 FAR = 7
 
@@ -210,101 +211,133 @@
             part[zc * 4 + column] = out.astype(jnp.bfloat16)
             if k < 2:
                 for a, j in (((0, 0), (1, 0)), ((0, 1),), ((1, 1),), ())[t]:
-                    firsts[a, k, j].start()
-
-    spans = [pl.ds(0, SIDE), pl.ds(SIDE, SIDE)]
-    both = pl.ds(0, 2 * SIDE)
+                    firsts[a, 0, k, j].start()
+
+    late_rows = EARLY * GROUP
+    wave_rows = [(late_rows, 2 * SIDE - late_rows), (0, late_rows)]
+    spans = [
+        [pl.ds(at, size // 2), pl.ds(at + size // 2, size // 2)] for at, size in wave_rows
+    ]
+    slots = [pl.ds(at // 2, size // 2) for at, size in wave_rows]
+    boths = [pl.ds(at, size) for at, size in wave_rows]
     last = pl.ds(2 * SIDE, LAST)
     last_spans = [pl.ds(2 * SIDE, LAST // 2), pl.ds(2 * SIDE + LAST // 2, LAST // 2)]
 
     def owner_of(k, yy, xx):
         return chunk_z(k) * 4 + yy * 2 + xx
 
-    def first_copy(axis, k, j):
+    def first_copy(axis, w, k, j):
         if axis == 0:
             owner = owner_of(k, 1 - y if j == 0 else y, 1 - x)
         else:
             owner = owner_of(k, 1 - y, 1 - x if j == 0 else x)
         return send(
-            part.at[owner, spans[axis]], first_in.at[axis, k, j],
-            first_send.at[axis, k, j], first_recv.at[axis, k, j],
+            part.at[owner, spans[w][axis]], first_in.at[axis, k, j, slots[w]],
+            first_send.at[axis, w, k, j], first_recv.at[axis, w, k, j],
             x_peer if axis == 0 else y_peer, mode,
         )
 
     def second_owner(axis, k):
         return owner_of(k, 1 - y, x) if axis == 0 else owner_of(k, y, 1 - x)
 
-    def second_copy(axis, k):
-        return send(
-            part.at[second_owner(axis, k), spans[axis]], second_in.at[axis, k],
-            second_send.at[axis, k], second_recv.at[axis, k],
+    def second_copy(axis, w, k):
+        return send(
+            part.at[second_owner(axis, k), spans[w][axis]], second_in.at[axis, k, slots[w]],
+            second_send.at[axis, w, k], second_recv.at[axis, w, k],
             y_peer if axis == 0 else x_peer, mode,
         )
 
-    firsts = {(a, k, j): first_copy(a, k, j) for a in range(2) for k in range(4) for j in range(2)}
-    seconds = {(a, k): second_copy(a, k) for a in range(2) for k in range(4)}
+    steps = [(w, k) for w in range(2) for k in range(4)]
+    firsts = {
+        (a, w, k, j): first_copy(a, w, k, j) for a in range(2) for w, k in steps for j in range(2)
+    }
+    seconds = {(a, w, k): second_copy(a, w, k) for a in range(2) for w, k in steps}
 
     def f32(value):
         return value.astype(jnp.float32)
 
-    def start_first(k):
+    def start_first(step):
+        w, k = steps[step]
         for j in range(2):
             for a in range(2):
-                firsts[a, k, j].start()
-
-    def forward(k):
+                firsts[a, w, k, j].start()
+
+    def forward(step):
+        w, k = steps[step]
         for a in range(2):
-            firsts[a, k, 0].wait_recv()
+            firsts[a, w, k, 0].wait_recv()
             owner = second_owner(a, k)
-            part[owner, spans[a]] = (
-                f32(part[owner, spans[a]]) + f32(first_in[a, k, 0])
+            span = spans[w][a]
+            part[owner, span] = (
+                f32(part[owner, span]) + f32(first_in[a, k, 0, slots[w]])
             ).astype(jnp.bfloat16)
-            seconds[a, k].start()
-
-    def line_copy(k, to):
+            seconds[a, w, k].start()
+
+    def line_copy(w, k, to):
         owner = owner_of(k, y, x)
+        both = boths[w]
         if to == "outer":
-            dst, sem = outer_in.at[k], outer_recv.at[k]
+            dst, sem = outer_in.at[k, both], outer_recv.at[w, k]
         elif to == "inner":
-            dst, sem = inner_in.at[k], inner_recv.at[k]
+            dst, sem = inner_in.at[k, both], inner_recv.at[w, k]
         else:
-            dst, sem = end_in, end_recv
-        return send(
-            part.at[owner, both], dst, line_send.at[k], sem,
+            dst, sem = end_in.at[both], end_recv.at[w]
+        return send(
+            part.at[owner, both], dst, line_send.at[w, k], sem,
             outer_peer if to == "end" else inner_peer, mode,
         )
 
-    def keep(k):
+    def keep(step):
+        w, k = steps[step]
         owner = owner_of(k, y, x)
         for a in range(2):
-            firsts[a, k, 1].wait_recv()
-            seconds[a, k].wait_recv()
+            firsts[a, w, k, 1].wait_recv()
+            seconds[a, w, k].wait_recv()
+            span = spans[w][a]
             value = (
-                f32(part[owner, spans[a]]) + f32(first_in[a, k, 1]) + f32(second_in[a, k])
+                f32(part[owner, span])
+                + f32(first_in[a, k, 1, slots[w]])
+                + f32(second_in[a, k, slots[w]])
             )
             if k >= 2:
                 @pl.when(is_mid if k == 2 else is_end)
                 def _():
-                    total[spans[a], :] = value
-            part[owner, spans[a]] = value.astype(jnp.bfloat16)
+                    total[span, :] = value
+            part[owner, span] = value.astype(jnp.bfloat16)
         if k < 3:
             @pl.when(is_end)
             def _():
-                line_copy(k, "outer").start()
-
-    def pass_on(k):
+                line_copy(w, k, "outer").start()
+
+    def pass_on(step):
+        w, k = steps[step]
         owner = owner_of(k, y, x)
+        both = boths[w]
 
         @pl.when(is_mid)
         def _():
             if k < 2:
-                line_copy(k, "outer").wait_recv()
-                arrived = outer_in[k]
+                line_copy(w, k, "outer").wait_recv()
+                arrived = outer_in[k, both]
             else:
-                line_copy(0, "inner").wait_recv()
-                arrived = inner_in[0]
+                line_copy(w, 0, "inner").wait_recv()
+                arrived = inner_in[0, both]
             part[owner, both] = (f32(part[owner, both]) + f32(arrived)).astype(jnp.bfloat16)
-            line_copy(k, "inner" if k < 2 else "end").start()
+            line_copy(w, k, "inner" if k < 2 else "end").start()
+
+    def line_end(w):
+        both = boths[w]
+
+        @pl.when(is_mid)
+        def _():
+            line_copy(w, 2, "outer").wait_recv()
+            line_copy(w, 1, "inner").wait_recv()
+            total[both, :] = total[both, :] + f32(outer_in[2, both]) + f32(inner_in[1, both])
+
+        @pl.when(is_end)
+        def _():
+            line_copy(w, 3, "end").wait_recv()
+            total[both, :] = total[both, :] + f32(end_in[both])
 
     def last_copy(k, to):
         owners = pl.ds(chunk_z(k) * 4, 4)
@@ -401,7 +434,6 @@
                 f32(part[pix, last_spans[a]]) + f32(last_first_in[a, 1]) + f32(last_second_in[a])
             )
 
-    rest = (FAR - 1) * GROUP
     ring = pix % 4 * 4 + z
 
     def chip_at(step):
@@ -415,8 +447,24 @@
             cross_send.at[index], cross_recv.at[index], pix, 1 - mode,
         )
 
-    cross_rest = cross_copy(0, rest, 0)
-    cross_early = cross_copy(rest, GROUP, 1)
+    cross_rows = [(FAR, FAR + 1), (EARLY, FAR), (1, EARLY)]
+    crosses = [
+        cross_copy((first - 1) * GROUP, (end - first) * GROUP, i)
+        for i, (first, end) in enumerate(cross_rows)
+    ]
+
+    def start_cross(i):
+        first, end = cross_rows[i]
+        cross_out[(first - 1) * GROUP:(end - 1) * GROUP] = total[
+            first * GROUP:end * GROUP, 128:256
+        ].astype(jnp.bfloat16)
+        crosses[i].start()
+
+    def mirror(i):
+        crosses[i].wait_recv()
+        for d in range(*cross_rows[i]):
+            start_turn(d)
+
     turns = [
         send(
             turn_out.at[d - 1], turn_in.at[d - 1], turn_send.at[d - 1], turn_recv.at[d - 1],
@@ -470,6 +518,7 @@
     ref_next(1)
     keep(0)
     forward(2)
+    start_first(4)
     last_pass(3)
     ref_next(2)
     last_spread()
@@ -477,31 +526,33 @@
     pass_on(0)
     ref_next(3)
     forward(3)
+    start_first(5)
     last_forward()
     keep(2)
     pass_on(1)
+    forward(4)
+    start_first(6)
     last_keep()
-    cross_out[rest:] = total[FAR * GROUP:NEAR * GROUP - GROUP, 128:256].astype(jnp.bfloat16)
-    cross_early.start()
+    start_cross(0)
     keep(3)
     pass_on(3)
-
-    cross_early.wait_recv()
-    start_turn(FAR)
-
-    @pl.when(is_mid)
-    def _():
-        line_copy(2, "outer").wait_recv()
-        line_copy(1, "inner").wait_recv()
-        total[both, :] = total[both, :] + f32(outer_in[2]) + f32(inner_in[1])
-
-    @pl.when(is_end)
-    def _():
-        line_copy(3, "end").wait_recv()
-        total[both, :] = total[both, :] + f32(end_in[...])
-
-    cross_out[0:rest] = total[GROUP:FAR * GROUP, 128:256].astype(jnp.bfloat16)
-    cross_rest.start()
+    forward(5)
+    start_first(7)
+    mirror(0)
+    keep(4)
+    forward(6)
+    line_end(0)
+    start_cross(1)
+    keep(5)
+    pass_on(4)
+    forward(7)
+    keep(6)
+    pass_on(5)
+    mirror(1)
+    keep(7)
+    pass_on(7)
+    line_end(1)
+    start_cross(2)
 
     lane = lax.broadcasted_iota(jnp.int32, (GROUP, 128), 1)
     low = lane < GROUP
@@ -515,9 +566,7 @@
         gram_ref[0, group_rows(d), :] = jnp.where(low, here, pltpu.roll(there, GROUP, 1))
         gram_ref[1, group_rows(d), :] = jnp.where(low, pltpu.roll(here, GROUP, 1), there)
 
-    cross_rest.wait_recv()
-    for d in range(1, FAR):
-        start_turn(d)
+    mirror(2)
     ref_copies[4].wait_recv()
     sums_ref[0] = ref_out[4]
     sums_ref[1] = ref_in[4]
@@ -529,17 +578,19 @@
 
     for copy in field_copies + ref_copies + list(firsts.values()) + list(seconds.values()):
         copy.wait_send()
-    for copy in turns + [cross_rest, cross_early] + list(last_firsts.values()) + last_seconds:
+    for copy in turns + crosses + list(last_firsts.values()) + last_seconds:
         copy.wait_send()
     for k in range(3):
         @pl.when(is_end | (k < 2))
         def _():
-            line_copy(k, "outer").wait_send()
+            line_copy(0, k, "outer").wait_send()
+            line_copy(1, k, "outer").wait_send()
             last_copy(k, "outer").wait_send()
 
     @pl.when(is_mid)
     def _():
-        line_copy(3, "end").wait_send()
+        line_copy(0, 3, "end").wait_send()
+        line_copy(1, 3, "end").wait_send()
         last_copy(3, "end").wait_send()
 
 
@@ -612,13 +663,13 @@
             pltpu.VMEM((FAR, 128, 128), b16),
             pltpu.VMEM((FAR, 128, 128), b16),
             dma((4,)), dma((4, 4)), dma((4, 4)),
-            dma((2, 4, 2)), dma((2, 4, 2)),
-            dma((2, 4)), dma((2, 4)),
-            dma((4,)), dma((3,)), dma((2,)), dma,
+            dma((2, 2, 4, 2)), dma((2, 2, 4, 2)),
+            dma((2, 2, 4)), dma((2, 2, 4)),
+            dma((2, 4)), dma((2, 3)), dma((2, 2)), dma((2,)),
             dma((4,)), dma((3,)), dma((2,)), dma,
             dma((2, 2)), dma((2, 2)), dma((2,)), dma((2,)),
             dma((5,)), dma((5,)),
-            dma((2,)), dma((2,)),
+            dma((3,)), dma((3,)),
             dma((FAR,)), dma((FAR,)),
         ],
         compiler_params=pltpu.CompilerParams(
@@ -631,6 +682,7 @@
         out_shape=(jax.ShapeDtypeStruct((2, GROUP, width), jnp.float32),) * 2,
         in_specs=[pl.BlockSpec(memory_space=pltpu.VMEM)] * 2,
         out_specs=(pl.BlockSpec(memory_space=pltpu.VMEM),) * 2,
+        compiler_params=pltpu.CompilerParams(vmem_limit_bytes=16 * 1024 * 1024),
     )(gram, sums)
     return (jnp.swapaxes(band, 1, 2), jnp.swapaxes(diag, 1, 2))
 

time: 67.2 us -> 68.1 us (1.013)
  Pallas kernels: 64.1 us -> 66.7 us
  local copies, waits for them, and re-layouts: 2.23 us -> 0.65 us
    pallas_call x1, Pallas kernels: 61.2 us -> 65 us  [paired_shards(): pl.pallas_call(gram_kernel, out_shape=(jax.ShapeDtypeStruct((2, width, 12...]
    unnamed x6 -> x2, local copies, waits for them, and re-layouts: 2.23 us -> 0.65 us
    pallas_call x1, Pallas kernels: 2.86 us -> 1.64 us  [paired_shards(): pl.pallas_call(functools.partial(finish_kernel, pixel_scale), out_shape=(...]
where the time goes in v5:
time: 68.1 us; the launch traced here: 68 us
  Pallas kernels  66.7 us (98%)
    pallas_call x1, Pallas kernels, paired_shards(): pl.pallas_call(gram_kernel, out_shape=(jax.ShapeDtypeStruct((2, width, 12...  65 us
    pallas_call x1, Pallas kernels, paired_shards(): pl.pallas_call(functools.partial(finish_kernel, pixel_scale), out_shape=(...  1.64 us

profile of v5, /device:TPU:0, one launch (start us, length us, event | category | flops | bytes accessed | tf_op | source)
XLA Modules:
  0.0 68.0 jit_solution(7819911189992367543)
XLA Ops:
  0.6 0.0 copy-start
  0.6 0.6 copy-done
  1.3 65.0 %shard_map.41 = (f32[2,1024,128]{2,1,0:T(8,128)S(1)}, f32[2,8,1024]{2,1,0:T(8,128)S(1)}) custom-call(bf16[4,512,1024]{2,1,0:T(8,128)(2,1)} %frames_hbm.1, s32[1,64]{1,0:T(1,128)S(1)} %bitcast.3), custom_call_target="tpu_custom_call" | custom-call | tf_op jit(solution)/shard_map/pallas_call | solution.py:632
  66.3 1.6 %shard_map.42 = (f32[2,64,1024]{2,1,0:T(8,128)}, f32[2,64,1024]{2,1,0:T(8,128)}) custom-call(f32[2,1024,128]{2,1,0:T(8,128)S(1)} %get-tuple-element.6.gram_ref, f32[2,8,1024]{2,1,0:T(8,128)S(1)} %get-tuple-element.7.sums_ref), custom_call_target="tpu_custom_call" | custom-call | tf_op jit(solution)/shard_map/pallas_call | solution.py:680
Async XLA Ops:
  0.6 0.7 copy-start

commit v6 on v4

--- a/solution.py
+++ b/solution.py
@@ -88,7 +88,8 @@
 GROUP = 64
 NEAR = 9
 SIDE = 224
-LAST = 128
+LAST = 96
+PACK = GROUP // 2
 FAR = 7
 
 
@@ -96,12 +97,12 @@
     frames_hbm, pixels_ref, gram_ref, sums_ref,
     frames_ref, own, other, part, first_in, second_in, outer_in, inner_in, end_in,
     last_outer_in, last_inner_in, last_end_in, last_first_in, last_second_in,
-    ref_out, ref_in, total, cross_out, cross_in, turn_out, turn_in,
+    ref_out, ref_in, total, cross_out, cross_in, turn_out, turn_in, shared_out, shared_in,
     frame_sem, field_send, field_recv, first_send, first_recv, second_send, second_recv,
     line_send, outer_recv, inner_recv, end_recv,
     last_send, last_outer_recv, last_inner_recv, last_end_recv,
     last_first_send, last_first_recv, last_second_send, last_second_recv, ref_send, ref_recv,
-    cross_send, cross_recv, turn_send, turn_recv,
+    cross_send, cross_recv, turn_send, turn_recv, shared_send, shared_recv,
 ):
     pix = lax.axis_index("pix")
     mode = lax.axis_index("mode")
@@ -118,6 +119,7 @@
     pixel_rows = frames_hbm.shape[1]
     width = frames_hbm.shape[2]
     rows = NEAR * GROUP
+    top = rows - GROUP
     chunk = 4 * GROUP
 
     def chunk_z(k):
@@ -140,6 +142,7 @@
             barrier, inc=1, device_id=((pix + step) % 16, mode), device_id_type=MESH
         )
     pl.semaphore_signal(barrier, inc=1, device_id=(pix, 1 - mode), device_id_type=MESH)
+    pl.semaphore_signal(barrier, inc=1, device_id=(y_peer, 1 - mode), device_id_type=MESH)
 
     def send(src, dst, send_sem, recv_sem, to_pix, to_mode):
         copy = pltpu.make_async_remote_copy(
@@ -161,7 +164,7 @@
             own[to, 0:pixel_rows] = real[i * GROUP:(i + 1) * GROUP]
             own[to, pixel_rows:2 * pixel_rows] = imag[i * GROUP:(i + 1) * GROUP]
     own[pl.ds(width, 8 * GROUP), :] = own[pl.ds(0, 8 * GROUP), :]
-    pl.semaphore_wait(barrier, 16)
+    pl.semaphore_wait(barrier, 17)
 
     def field_copy(k, i):
         at = ring_rows(chunk_z(k), i)
@@ -207,7 +210,12 @@
             )
             left = own[pl.ds(start, rows), :]
             out = lax.dot_general(left, cols, contract, preferred_element_type=jnp.float32)
-            part[zc * 4 + column] = out.astype(jnp.bfloat16)
+            part[zc * 4 + column, pl.ds(0, top)] = out[:top].astype(jnp.bfloat16)
+            owner_y = 1 - y if t % 2 == 0 else y
+            shared = jnp.where(owner_y == 0, out[top:, 0:128], out[top:, 128:256])
+            part[zc * 4 + column, pl.ds(top, PACK)] = jnp.concatenate(
+                [shared[:PACK], shared[PACK:]], axis=1
+            ).astype(jnp.bfloat16)
             if k < 2:
                 for a, j in (((0, 0), (1, 0)), ((0, 1),), ((1, 1),), ())[t]:
                     firsts[a, k, j].start()
@@ -417,6 +425,10 @@
 
     cross_rest = cross_copy(0, rest, 0)
     cross_early = cross_copy(rest, GROUP, 1)
+    shared_copy = send(
+        shared_out, shared_in, shared_send, shared_recv,
+        y_peer, jnp.where(y == 0, mode, 1 - mode),
+    )
     turns = [
         send(
             turn_out.at[d - 1], turn_in.at[d - 1], turn_send.at[d - 1], turn_recv.at[d - 1],
@@ -483,6 +495,11 @@
     last_keep()
     cross_out[rest:] = total[FAR * GROUP:NEAR * GROUP - GROUP, 128:256].astype(jnp.bfloat16)
     cross_early.start()
+    shared = jnp.concatenate(
+        [total[top:top + PACK, 0:128], total[top:top + PACK, 128:256]], axis=0
+    )
+    shared_out[...] = jnp.concatenate([shared, shared], axis=0).astype(jnp.bfloat16).T
+    shared_copy.start()
     keep(3)
     pass_on(3)
 
@@ -509,7 +526,7 @@
     def group_rows(step):
         return pl.ds(pl.multiple_of(chip_at(step) * GROUP, GROUP), GROUP)
 
-    for d in range(NEAR):
+    for d in range(NEAR - 1):
         here = total[d * GROUP:(d + 1) * GROUP, 0:128]
         there = total[d * GROUP:(d + 1) * GROUP, 128:256]
         gram_ref[0, group_rows(d), :] = jnp.where(low, here, pltpu.roll(there, GROUP, 1))
@@ -518,6 +535,19 @@
     cross_rest.wait_recv()
     for d in range(1, FAR):
         start_turn(d)
+    shared_copy.wait_recv()
+    arrived = f32(shared_in[...])
+    mine = low == (y == 0)
+    shared = jnp.concatenate(
+        [total[top:top + PACK, 0:128], total[top:top + PACK, 128:256]], axis=0
+    )
+    rolled = pltpu.roll(shared, GROUP, 1)
+    gram_ref[0, group_rows(8), :] = jnp.where(
+        mine, jnp.where(low, shared, rolled), arrived[0:GROUP]
+    )
+    gram_ref[1, group_rows(8), :] = jnp.where(
+        mine, jnp.where(low, rolled, shared), -arrived[GROUP:]
+    )
     ref_copies[4].wait_recv()
     sums_ref[0] = ref_out[4]
     sums_ref[1] = ref_in[4]
@@ -529,7 +559,7 @@
 
     for copy in field_copies + ref_copies + list(firsts.values()) + list(seconds.values()):
         copy.wait_send()
-    for copy in turns + [cross_rest, cross_early] + list(last_firsts.values()) + last_seconds:
+    for copy in turns + [cross_rest, cross_early, shared_copy] + list(last_firsts.values()) + last_seconds:
         copy.wait_send()
     for k in range(3):
         @pl.when(is_end | (k < 2))
@@ -575,7 +605,7 @@
 def paired_shards(frames, ref_pixels):
     pixel_rows = frames.shape[1]
     width = frames.shape[2]
-    rows = NEAR * GROUP
+    rows = 2 * SIDE + LAST
     b16 = jnp.bfloat16
     dma = pltpu.SemaphoreType.DMA
     gram, sums = pl.pallas_call(
@@ -611,6 +641,8 @@
             pltpu.VMEM((FAR * GROUP, 128), b16),
             pltpu.VMEM((FAR, 128, 128), b16),
             pltpu.VMEM((FAR, 128, 128), b16),
+            pltpu.VMEM((128, 128), b16),
+            pltpu.VMEM((128, 128), b16),
             dma((4,)), dma((4, 4)), dma((4, 4)),
             dma((2, 4, 2)), dma((2, 4, 2)),
             dma((2, 4)), dma((2, 4)),
@@ -620,6 +652,7 @@
             dma((5,)), dma((5,)),
             dma((2,)), dma((2,)),
             dma((FAR,)), dma((FAR,)),
+            dma, dma,
         ],
         compiler_params=pltpu.CompilerParams(
             collective_id=0, has_side_effects=True, vmem_limit_bytes=52 * 1024 * 1024
@@ -631,6 +664,7 @@
         out_shape=(jax.ShapeDtypeStruct((2, GROUP, width), jnp.float32),) * 2,
         in_specs=[pl.BlockSpec(memory_space=pltpu.VMEM)] * 2,
         out_specs=(pl.BlockSpec(memory_space=pltpu.VMEM),) * 2,
+        compiler_params=pltpu.CompilerParams(vmem_limit_bytes=16 * 1024 * 1024),
     )(gram, sums)
     return (jnp.swapaxes(band, 1, 2), jnp.swapaxes(diag, 1, 2))
 

time: 67.2 us -> 63.6 us (0.946)
  Pallas kernels: 64.1 us -> 62.2 us
  local copies, waits for them, and re-layouts: 2.23 us -> 0.65 us
    unnamed x6 -> x2, local copies, waits for them, and re-layouts: 2.23 us -> 0.65 us
    pallas_call x1, Pallas kernels: 2.86 us -> 1.64 us  [paired_shards(): pl.pallas_call(functools.partial(finish_kernel, pixel_scale), out_shape=(...]
    pallas_call x1, Pallas kernels: 61.2 us -> 60.5 us  [paired_shards(): pl.pallas_call(gram_kernel, out_shape=(jax.ShapeDtypeStruct((2, width, 12...]
where the time goes in v6:
time: 63.6 us; the launch traced here: 63.5 us
  Pallas kernels  62.2 us (98%)
  local copies, waits for them, and re-layouts  0.65 us (1%)
  between operations  0.65 us (1%)
    pallas_call x1, Pallas kernels, paired_shards(): pl.pallas_call(gram_kernel, out_shape=(jax.ShapeDtypeStruct((2, width, 12...  60.5 us
    pallas_call x1, Pallas kernels, paired_shards(): pl.pallas_call(functools.partial(finish_kernel, pixel_scale), out_shape=(...  1.64 us

profile of v6, /device:TPU:0, one launch (start us, length us, event | category | flops | bytes accessed | tf_op | source)
XLA Modules:
  0.0 63.5 jit_solution(2487906573432731478)
XLA Ops:
  0.6 0.0 copy-start
  0.6 0.6 %copy-done = s32[64]{0:T(128)S(1)} copy-done((s32[64]{0:T(128)S(1)}, s32[64]{0:T(128)}, u32[]{:S(2)}) %copy-start) | copy-done | bytes 280
  1.3 60.5 %shard_map.41 = (f32[2,1024,128]{2,1,0:T(8,128)S(1)}, f32[2,8,1024]{2,1,0:T(8,128)S(1)}) custom-call(bf16[4,512,1024]{2,1,0:T(8,128)(2,1)} %frames_hbm.1, s32[1,64]{1,0:T(1,128)S(1)} %bitcast.3), custom_call_target="tpu_custom_call" | custom-call | tf_op jit(solution)/shard_map/pallas_call | solution.py:611
  61.8 1.6 %shard_map.42 = (f32[2,64,1024]{2,1,0:T(8,128)}, f32[2,64,1024]{2,1,0:T(8,128)}) custom-call(f32[2,1024,128]{2,1,0:T(8,128)S(1)} %get-tuple-element.6.gram_ref, f32[2,8,1024]{2,1,0:T(8,128)S(1)} %get-tuple-element.7.sums_ref), custom_call_target="tpu_custom_call" | custom-call | tf_op jit(solution)/shard_map/pallas_call | solution.py:662
Async XLA Ops:
  0.6 0.7 %copy-start = (s32[64]{0:T(128)S(1)}, s32[64]{0:T(128)}, u32[]{:S(2)}) copy-start(s32[64]{0:T(128)} %param.3) | copy-start | bytes 772

commit v7 on v6

--- a/solution.py
+++ b/solution.py
@@ -94,11 +94,11 @@
 
 
 def gram_kernel(
-    frames_hbm, pixels_ref, gram_ref, sums_ref,
-    frames_ref, own, other, part, first_in, second_in, outer_in, inner_in, end_in,
+    frames_hbm, pixels_hbm, gram_ref, sums_ref,
+    pixels_ref, frames_ref, own, other, part, first_in, second_in, outer_in, inner_in, end_in,
     last_outer_in, last_inner_in, last_end_in, last_first_in, last_second_in,
     ref_out, ref_in, total, cross_out, cross_in, turn_out, turn_in, shared_out, shared_in,
-    frame_sem, field_send, field_recv, first_send, first_recv, second_send, second_recv,
+    pixel_sem, frame_sem, field_send, field_recv, first_send, first_recv, second_send, second_recv,
     line_send, outer_recv, inner_recv, end_recv,
     last_send, last_outer_recv, last_inner_recv, last_end_recv,
     last_first_send, last_first_recv, last_second_send, last_second_recv, ref_send, ref_recv,
@@ -136,6 +136,8 @@
     ]
     for load in loads:
         load.start()
+    listing = pltpu.make_async_copy(pixels_hbm, pixels_ref, pixel_sem)
+    listing.start()
     barrier = pltpu.get_barrier_semaphore()
     for step in range(1, 16):
         pl.semaphore_signal(
@@ -221,7 +223,6 @@
                     firsts[a, k, j].start()
 
     spans = [pl.ds(0, SIDE), pl.ds(SIDE, SIDE)]
-    both = pl.ds(0, 2 * SIDE)
     last = pl.ds(2 * SIDE, LAST)
     last_spans = [pl.ds(2 * SIDE, LAST // 2), pl.ds(2 * SIDE + LAST // 2, LAST // 2)]
 
@@ -269,50 +270,67 @@
             ).astype(jnp.bfloat16)
             seconds[a, k].start()
 
-    def line_copy(k, to):
+    def line_copy(k, a, to):
         owner = owner_of(k, y, x)
+        span = spans[a]
         if to == "outer":
-            dst, sem = outer_in.at[k], outer_recv.at[k]
+            dst, sem = outer_in.at[k, span], outer_recv.at[k, a]
         elif to == "inner":
-            dst, sem = inner_in.at[k], inner_recv.at[k]
+            dst, sem = inner_in.at[k, span], inner_recv.at[k, a]
         else:
-            dst, sem = end_in, end_recv
-        return send(
-            part.at[owner, both], dst, line_send.at[k], sem,
+            dst, sem = end_in.at[span], end_recv.at[a]
+        return send(
+            part.at[owner, span], dst, line_send.at[k, a], sem,
             outer_peer if to == "end" else inner_peer, mode,
         )
 
     def keep(k):
         owner = owner_of(k, y, x)
-        for a in range(2):
+        for a in (1, 0):
             firsts[a, k, 1].wait_recv()
             seconds[a, k].wait_recv()
-            value = (
-                f32(part[owner, spans[a]]) + f32(first_in[a, k, 1]) + f32(second_in[a, k])
-            )
+            span = spans[a]
+            value = f32(part[owner, span]) + f32(first_in[a, k, 1]) + f32(second_in[a, k])
             if k >= 2:
                 @pl.when(is_mid if k == 2 else is_end)
                 def _():
-                    total[spans[a], :] = value
-            part[owner, spans[a]] = value.astype(jnp.bfloat16)
-        if k < 3:
-            @pl.when(is_end)
-            def _():
-                line_copy(k, "outer").start()
-
-    def pass_on(k):
+                    total[span, :] = value
+            part[owner, span] = value.astype(jnp.bfloat16)
+            if k < 3:
+                @pl.when(is_end)
+                def _():
+                    line_copy(k, a, "outer").start()
+            else:
+                pass_on(k, a)
+
+    def pass_on(k, a):
         owner = owner_of(k, y, x)
+        span = spans[a]
 
         @pl.when(is_mid)
         def _():
             if k < 2:
-                line_copy(k, "outer").wait_recv()
-                arrived = outer_in[k]
+                line_copy(k, a, "outer").wait_recv()
+                arrived = outer_in[k, span]
             else:
-                line_copy(0, "inner").wait_recv()
-                arrived = inner_in[0]
-            part[owner, both] = (f32(part[owner, both]) + f32(arrived)).astype(jnp.bfloat16)
-            line_copy(k, "inner" if k < 2 else "end").start()
+                line_copy(0, a, "inner").wait_recv()
+                arrived = inner_in[0, span]
+            part[owner, span] = (f32(part[owner, span]) + f32(arrived)).astype(jnp.bfloat16)
+            line_copy(k, a, "inner" if k < 2 else "end").start()
+
+    def line_end(a):
+        span = spans[a]
+
+        @pl.when(is_mid)
+        def _():
+            line_copy(2, a, "outer").wait_recv()
+            line_copy(1, a, "inner").wait_recv()
+            total[span, :] = total[span, :] + f32(outer_in[2, span]) + f32(inner_in[1, span])
+
+        @pl.when(is_end)
+        def _():
+            line_copy(3, a, "end").wait_recv()
+            total[span, :] = total[span, :] + f32(end_in[span])
 
     def last_copy(k, to):
         owners = pl.ds(chunk_z(k) * 4, 4)
@@ -409,7 +427,6 @@
                 f32(part[pix, last_spans[a]]) + f32(last_first_in[a, 1]) + f32(last_second_in[a])
             )
 
-    rest = (FAR - 1) * GROUP
     ring = pix % 4 * 4 + z
 
     def chip_at(step):
@@ -423,8 +440,24 @@
             cross_send.at[index], cross_recv.at[index], pix, 1 - mode,
         )
 
-    cross_rest = cross_copy(0, rest, 0)
-    cross_early = cross_copy(rest, GROUP, 1)
+    cross_rows = [(FAR, FAR + 1), (4, FAR), (1, 4)]
+    crosses = [
+        cross_copy((first - 1) * GROUP, (end - first) * GROUP, i)
+        for i, (first, end) in enumerate(cross_rows)
+    ]
+
+    def start_cross(i):
+        first, end = cross_rows[i]
+        cross_out[(first - 1) * GROUP:(end - 1) * GROUP] = total[
+            first * GROUP:end * GROUP, 128:256
+        ].astype(jnp.bfloat16)
+        crosses[i].start()
+
+    def mirror(i):
+        crosses[i].wait_recv()
+        for d in range(*cross_rows[i]):
+            start_turn(d)
+
     shared_copy = send(
         shared_out, shared_in, shared_send, shared_recv,
         y_peer, jnp.where(y == 0, mode, 1 - mode),
@@ -454,6 +487,7 @@
     positions = pix * pixel_rows + lax.broadcasted_iota(
         jnp.int32, (pixels_ref.shape[1], pixel_rows), 1
     )
+    listing.wait()
     listed = jnp.broadcast_to(pixels_ref[...], (8, pixels_ref.shape[1])).T[:, 0:1]
     counts = jnp.sum(
         jnp.where(listed == positions, 1.0, 0.0), axis=0, keepdims=True
@@ -486,39 +520,25 @@
     ref_next(2)
     last_spread()
     keep(1)
-    pass_on(0)
+    pass_on(0, 1)
+    pass_on(0, 0)
     ref_next(3)
     forward(3)
     last_forward()
     keep(2)
-    pass_on(1)
+    pass_on(1, 1)
+    pass_on(1, 0)
     last_keep()
-    cross_out[rest:] = total[FAR * GROUP:NEAR * GROUP - GROUP, 128:256].astype(jnp.bfloat16)
-    cross_early.start()
+    start_cross(0)
     shared = jnp.concatenate(
         [total[top:top + PACK, 0:128], total[top:top + PACK, 128:256]], axis=0
     )
     shared_out[...] = jnp.concatenate([shared, shared], axis=0).astype(jnp.bfloat16).T
     shared_copy.start()
     keep(3)
-    pass_on(3)
-
-    cross_early.wait_recv()
-    start_turn(FAR)
-
-    @pl.when(is_mid)
-    def _():
-        line_copy(2, "outer").wait_recv()
-        line_copy(1, "inner").wait_recv()
-        total[both, :] = total[both, :] + f32(outer_in[2]) + f32(inner_in[1])
-
-    @pl.when(is_end)
-    def _():
-        line_copy(3, "end").wait_recv()
-        total[both, :] = total[both, :] + f32(end_in[...])
-
-    cross_out[0:rest] = total[GROUP:FAR * GROUP, 128:256].astype(jnp.bfloat16)
-    cross_rest.start()
+    mirror(0)
+    line_end(1)
+    start_cross(1)
 
     lane = lax.broadcasted_iota(jnp.int32, (GROUP, 128), 1)
     low = lane < GROUP
@@ -526,15 +546,18 @@
     def group_rows(step):
         return pl.ds(pl.multiple_of(chip_at(step) * GROUP, GROUP), GROUP)
 
-    for d in range(NEAR - 1):
+    def place(d):
         here = total[d * GROUP:(d + 1) * GROUP, 0:128]
         there = total[d * GROUP:(d + 1) * GROUP, 128:256]
         gram_ref[0, group_rows(d), :] = jnp.where(low, here, pltpu.roll(there, GROUP, 1))
         gram_ref[1, group_rows(d), :] = jnp.where(low, pltpu.roll(here, GROUP, 1), there)
 
-    cross_rest.wait_recv()
-    for d in range(1, FAR):
-        start_turn(d)
+    mirror(1)
+    line_end(0)
+    start_cross(2)
+    for d in range(NEAR - 1):
+        place(d)
+    mirror(2)
     shared_copy.wait_recv()
     arrived = f32(shared_in[...])
     mine = low == (y == 0)
@@ -559,17 +582,19 @@
 
     for copy in field_copies + ref_copies + list(firsts.values()) + list(seconds.values()):
         copy.wait_send()
-    for copy in turns + [cross_rest, cross_early, shared_copy] + list(last_firsts.values()) + last_seconds:
+    for copy in turns + crosses + [shared_copy] + list(last_firsts.values()) + last_seconds:
         copy.wait_send()
     for k in range(3):
         @pl.when(is_end | (k < 2))
         def _():
-            line_copy(k, "outer").wait_send()
+            line_copy(k, 0, "outer").wait_send()
+            line_copy(k, 1, "outer").wait_send()
             last_copy(k, "outer").wait_send()
 
     @pl.when(is_mid)
     def _():
-        line_copy(3, "end").wait_send()
+        line_copy(3, 0, "end").wait_send()
+        line_copy(3, 1, "end").wait_send()
         last_copy(3, "end").wait_send()
 
 
@@ -616,10 +641,11 @@
         ),
         in_specs=[
             pl.BlockSpec(memory_space=pltpu.HBM),
-            pl.BlockSpec(memory_space=pltpu.VMEM),
+            pl.BlockSpec(memory_space=pltpu.HBM),
         ],
         out_specs=(pl.BlockSpec(memory_space=pltpu.VMEM),) * 2,
         scratch_shapes=[
+            pltpu.VMEM((1, ref_pixels.shape[0]), jnp.int32),
             pltpu.VMEM((4, 4, pixel_rows, 4 * GROUP), b16),
             pltpu.VMEM((width + 8 * GROUP, 2 * pixel_rows), b16),
             pltpu.VMEM((width, 2 * pixel_rows), b16),
@@ -643,14 +669,14 @@
             pltpu.VMEM((FAR, 128, 128), b16),
             pltpu.VMEM((128, 128), b16),
             pltpu.VMEM((128, 128), b16),
-            dma((4,)), dma((4, 4)), dma((4, 4)),
+            dma, dma((4,)), dma((4, 4)), dma((4, 4)),
             dma((2, 4, 2)), dma((2, 4, 2)),
             dma((2, 4)), dma((2, 4)),
-            dma((4,)), dma((3,)), dma((2,)), dma,
+            dma((4, 2)), dma((3, 2)), dma((2, 2)), dma((2,)),
             dma((4,)), dma((3,)), dma((2,)), dma,
             dma((2, 2)), dma((2, 2)), dma((2,)), dma((2,)),
             dma((5,)), dma((5,)),
-            dma((2,)), dma((2,)),
+            dma((3,)), dma((3,)),
             dma((FAR,)), dma((FAR,)),
             dma, dma,
         ],

time: 63.6 us -> 61.3 us (0.964)
  Pallas kernels: 62.2 us -> 59.8 us
    pallas_call x1, Pallas kernels: 60.5 us -> 58.1 us  [paired_shards(): pl.pallas_call(gram_kernel, out_shape=(jax.ShapeDtypeStruct((2, width, 12...]
where the time goes in v7:
time: 61.3 us; the launch traced here: 61.1 us
  Pallas kernels  59.8 us (98%)
  local copies, waits for them, and re-layouts  0.65 us (1%)
  between operations  0.65 us (1%)
    pallas_call x1, Pallas kernels, paired_shards(): pl.pallas_call(gram_kernel, out_shape=(jax.ShapeDtypeStruct((2, width, 12...  58.1 us
    pallas_call x1, Pallas kernels, paired_shards(): pl.pallas_call(functools.partial(finish_kernel, pixel_scale), out_shape=(...  1.64 us

profile of v7, /device:TPU:0, one launch (start us, length us, event | category | flops | bytes accessed | tf_op | source)
XLA Modules:
  0.0 61.1 jit_solution(10157386578664765548)
XLA Ops:
  0.6 0.0 copy-start
  0.6 0.6 %copy-done = s32[64]{0:T(128)S(1)} copy-done((s32[64]{0:T(128)S(1)}, s32[64]{0:T(128)}, u32[]{:S(2)}) %copy-start) | copy-done | bytes 280
  1.3 58.1 %shard_map.41 = (f32[2,1024,128]{2,1,0:T(8,128)S(1)}, f32[2,8,1024]{2,1,0:T(8,128)S(1)}) custom-call(bf16[4,512,1024]{2,1,0:T(8,128)(2,1)} %frames_hbm.1, s32[1,64]{1,0:T(1,128)S(1)} %bitcast.3), custom_call_target="tpu_custom_call" | custom-call | tf_op jit(solution)/shard_map/pallas_call | solution.py:636
  59.4 1.6 %shard_map.42 = (f32[2,64,1024]{2,1,0:T(8,128)}, f32[2,64,1024]{2,1,0:T(8,128)}) custom-call(f32[2,1024,128]{2,1,0:T(8,128)S(1)} %get-tuple-element.6.gram_ref, f32[2,8,1024]{2,1,0:T(8,128)S(1)} %get-tuple-element.7.sums_ref), custom_call_target="tpu_custom_call" | custom-call | tf_op jit(solution)/shard_map/pallas_call | solution.py:688
Async XLA Ops:
  0.6 0.7 %copy-start = (s32[64]{0:T(128)S(1)}, s32[64]{0:T(128)}, u32[]{:S(2)}) copy-start(s32[64]{0:T(128)} %param.3) | copy-start | bytes 772

commit v8 on v7

--- a/solution.py
+++ b/solution.py
@@ -97,12 +97,12 @@
     frames_hbm, pixels_hbm, gram_ref, sums_ref,
     pixels_ref, frames_ref, own, other, part, first_in, second_in, outer_in, inner_in, end_in,
     last_outer_in, last_inner_in, last_end_in, last_first_in, last_second_in,
-    ref_out, ref_in, total, cross_out, cross_in, turn_out, turn_in, shared_out, shared_in,
+    ref_out, ref_in, total, turn_out, turn_in, shared_out, shared_in,
     pixel_sem, frame_sem, field_send, field_recv, first_send, first_recv, second_send, second_recv,
     line_send, outer_recv, inner_recv, end_recv,
     last_send, last_outer_recv, last_inner_recv, last_end_recv,
     last_first_send, last_first_recv, last_second_send, last_second_recv, ref_send, ref_recv,
-    cross_send, cross_recv, turn_send, turn_recv, shared_send, shared_recv,
+    turn_send, turn_recv, shared_send, shared_recv,
 ):
     pix = lax.axis_index("pix")
     mode = lax.axis_index("mode")
@@ -140,11 +140,11 @@
     listing.start()
     barrier = pltpu.get_barrier_semaphore()
     for step in range(1, 16):
-        pl.semaphore_signal(
-            barrier, inc=1, device_id=((pix + step) % 16, mode), device_id_type=MESH
-        )
+        for to_mode in (mode, 1 - mode):
+            pl.semaphore_signal(
+                barrier, inc=1, device_id=((pix + step) % 16, to_mode), device_id_type=MESH
+            )
     pl.semaphore_signal(barrier, inc=1, device_id=(pix, 1 - mode), device_id_type=MESH)
-    pl.semaphore_signal(barrier, inc=1, device_id=(y_peer, 1 - mode), device_id_type=MESH)
 
     def send(src, dst, send_sem, recv_sem, to_pix, to_mode):
         copy = pltpu.make_async_remote_copy(
@@ -166,7 +166,7 @@
             own[to, 0:pixel_rows] = real[i * GROUP:(i + 1) * GROUP]
             own[to, pixel_rows:2 * pixel_rows] = imag[i * GROUP:(i + 1) * GROUP]
     own[pl.ds(width, 8 * GROUP), :] = own[pl.ds(0, 8 * GROUP), :]
-    pl.semaphore_wait(barrier, 17)
+    pl.semaphore_wait(barrier, 31)
 
     def field_copy(k, i):
         at = ring_rows(chunk_z(k), i)
@@ -433,53 +433,33 @@
         there = (ring + step) % 16
         return there % 4 * 4 + there // 4
 
-    def cross_copy(at, size, index):
-        rows_at = pl.ds(at, size)
-        return send(
-            cross_out.at[rows_at], cross_in.at[rows_at],
-            cross_send.at[index], cross_recv.at[index], pix, 1 - mode,
-        )
-
-    cross_rows = [(FAR, FAR + 1), (4, FAR), (1, 4)]
-    crosses = [
-        cross_copy((first - 1) * GROUP, (end - first) * GROUP, i)
-        for i, (first, end) in enumerate(cross_rows)
-    ]
-
-    def start_cross(i):
-        first, end = cross_rows[i]
-        cross_out[(first - 1) * GROUP:(end - 1) * GROUP] = total[
-            first * GROUP:end * GROUP, 128:256
-        ].astype(jnp.bfloat16)
-        crosses[i].start()
+    mirror_rows = [(FAR, FAR + 1), (4, FAR), (1, 4)]
 
     def mirror(i):
-        crosses[i].wait_recv()
-        for d in range(*cross_rows[i]):
-            start_turn(d)
+        for d in range(*mirror_rows[i]):
+            for rel in range(2):
+                block = total[
+                    d * GROUP:(d + 1) * GROUP, rel * 128:(rel + 1) * 128
+                ].astype(jnp.bfloat16)
+                stacked = jnp.concatenate([block[:, :GROUP], block[:, GROUP:]], axis=0)
+                turn_out[d - 1, rel] = stacked.T
+                turns[d - 1][rel].start()
 
     shared_copy = send(
         shared_out, shared_in, shared_send, shared_recv,
         y_peer, jnp.where(y == 0, mode, 1 - mode),
     )
     turns = [
-        send(
-            turn_out.at[d - 1], turn_in.at[d - 1], turn_send.at[d - 1], turn_recv.at[d - 1],
-            chip_at(d), mode,
-        )
+        [
+            send(
+                turn_out.at[d - 1, rel], turn_in.at[d - 1, rel],
+                turn_send.at[d - 1, rel], turn_recv.at[d - 1, rel],
+                chip_at(d), mode if rel == 0 else 1 - mode,
+            )
+            for rel in range(2)
+        ]
         for d in range(1, FAR + 1)
     ]
-
-    def start_turn(d):
-        stacked = jnp.concatenate(
-            [
-                total[d * GROUP:(d + 1) * GROUP, 0:128].astype(jnp.bfloat16),
-                cross_in[(d - 1) * GROUP:d * GROUP, :],
-            ],
-            axis=0,
-        )
-        turn_out[d - 1] = stacked.T
-        turns[d - 1].start()
 
     for k in range(3):
         multiply(k)
@@ -529,16 +509,15 @@
     pass_on(1, 1)
     pass_on(1, 0)
     last_keep()
-    start_cross(0)
+    mirror(0)
     shared = jnp.concatenate(
         [total[top:top + PACK, 0:128], total[top:top + PACK, 128:256]], axis=0
     )
     shared_out[...] = jnp.concatenate([shared, shared], axis=0).astype(jnp.bfloat16).T
     shared_copy.start()
     keep(3)
-    mirror(0)
     line_end(1)
-    start_cross(1)
+    mirror(1)
 
     lane = lax.broadcasted_iota(jnp.int32, (GROUP, 128), 1)
     low = lane < GROUP
@@ -552,12 +531,10 @@
         gram_ref[0, group_rows(d), :] = jnp.where(low, here, pltpu.roll(there, GROUP, 1))
         gram_ref[1, group_rows(d), :] = jnp.where(low, pltpu.roll(here, GROUP, 1), there)
 
-    mirror(1)
     line_end(0)
-    start_cross(2)
+    mirror(2)
     for d in range(NEAR - 1):
         place(d)
-    mirror(2)
     shared_copy.wait_recv()
     arrived = f32(shared_in[...])
     mine = low == (y == 0)
@@ -575,14 +552,16 @@
     sums_ref[0] = ref_out[4]
     sums_ref[1] = ref_in[4]
     for d in range(1, FAR + 1):
-        turns[d - 1].wait_recv()
-        arrived = f32(turn_in[d - 1])
-        gram_ref[0, group_rows(16 - d), :] = arrived[0:GROUP]
-        gram_ref[1, group_rows(16 - d), :] = -arrived[GROUP:]
+        for rel in range(2):
+            turns[d - 1][rel].wait_recv()
+        here = f32(turn_in[d - 1, 0])
+        there = f32(turn_in[d - 1, 1])
+        gram_ref[0, group_rows(16 - d), :] = jnp.where(low, here, pltpu.roll(there, GROUP, 1))
+        gram_ref[1, group_rows(16 - d), :] = -jnp.where(low, pltpu.roll(here, GROUP, 1), there)
 
     for copy in field_copies + ref_copies + list(firsts.values()) + list(seconds.values()):
         copy.wait_send()
-    for copy in turns + crosses + [shared_copy] + list(last_firsts.values()) + last_seconds:
+    for copy in sum(turns, []) + [shared_copy] + list(last_firsts.values()) + last_seconds:
         copy.wait_send()
     for k in range(3):
         @pl.when(is_end | (k < 2))
@@ -663,10 +642,8 @@
             pltpu.VMEM((5, 8, width), jnp.float32),
             pltpu.VMEM((5, 8, width), jnp.float32),
             pltpu.VMEM((rows, 256), jnp.float32),
-            pltpu.VMEM((FAR * GROUP, 128), b16),
-            pltpu.VMEM((FAR * GROUP, 128), b16),
-            pltpu.VMEM((FAR, 128, 128), b16),
-            pltpu.VMEM((FAR, 128, 128), b16),
+            pltpu.VMEM((FAR, 2, GROUP, 128), b16),
+            pltpu.VMEM((FAR, 2, GROUP, 128), b16),
             pltpu.VMEM((128, 128), b16),
             pltpu.VMEM((128, 128), b16),
             dma, dma((4,)), dma((4, 4)), dma((4, 4)),
@@ -676,8 +653,7 @@
             dma((4,)), dma((3,)), dma((2,)), dma,
             dma((2, 2)), dma((2, 2)), dma((2,)), dma((2,)),
             dma((5,)), dma((5,)),
-            dma((3,)), dma((3,)),
-            dma((FAR,)), dma((FAR,)),
+            dma((FAR, 2)), dma((FAR, 2)),
             dma, dma,
         ],
         compiler_params=pltpu.CompilerParams(

time: 61.3 us -> 61.4 us (level)
  no operation moved by 1% of the time
where the time goes in v8:
time: 61.4 us; the launch traced here: 61.2 us
  Pallas kernels  60 us (98%)
  local copies, waits for them, and re-layouts  0.65 us (1%)
  between operations  0.65 us (1%)
    pallas_call x1, Pallas kernels, paired_shards(): pl.pallas_call(gram_kernel, out_shape=(jax.ShapeDtypeStruct((2, width, 12...  58.3 us
    pallas_call x1, Pallas kernels, paired_shards(): pl.pallas_call(functools.partial(finish_kernel, pixel_scale), out_shape=(...  1.64 us

profile of v8, /device:TPU:0, one launch (start us, length us, event | category | flops | bytes accessed | tf_op | source)
XLA Modules:
  0.0 61.2 jit_solution(8300863333903414465)
XLA Ops:
  0.6 0.0 copy-start
  0.6 0.6 %copy-done = s32[64]{0:T(128)S(1)} copy-done((s32[64]{0:T(128)S(1)}, s32[64]{0:T(128)}, u32[]{:S(2)}) %copy-start) | copy-done | bytes 280
  1.3 58.3 %shard_map.41 = (f32[2,1024,128]{2,1,0:T(8,128)S(1)}, f32[2,8,1024]{2,1,0:T(8,128)S(1)}) custom-call(bf16[4,512,1024]{2,1,0:T(8,128)(2,1)} %frames_hbm.1, s32[1,64]{1,0:T(1,128)S(1)} %bitcast.3), custom_call_target="tpu_custom_call" | custom-call | tf_op jit(solution)/shard_map/pallas_call | solution.py:615
  59.6 1.6 %shard_map.42 = (f32[2,64,1024]{2,1,0:T(8,128)}, f32[2,64,1024]{2,1,0:T(8,128)}) custom-call(f32[2,1024,128]{2,1,0:T(8,128)S(1)} %get-tuple-element.6.gram_ref, f32[2,8,1024]{2,1,0:T(8,128)S(1)} %get-tuple-element.7.sums_ref), custom_call_target="tpu_custom_call" | custom-call | tf_op jit(solution)/shard_map/pallas_call | solution.py:664
Async XLA Ops:
  0.6 0.7 %copy-start = (s32[64]{0:T(128)S(1)}, s32[64]{0:T(128)}, u32[]{:S(2)}) copy-start(s32[64]{0:T(128)} %param.3) | copy-start | bytes 772

commit v9 on v7

--- a/solution.py
+++ b/solution.py
@@ -218,7 +218,7 @@
             part[zc * 4 + column, pl.ds(top, PACK)] = jnp.concatenate(
                 [shared[:PACK], shared[PACK:]], axis=1
             ).astype(jnp.bfloat16)
-            if k < 2:
+            if k < 3:
                 for a, j in (((0, 0), (1, 0)), ((0, 1),), ((1, 1),), ())[t]:
                     firsts[a, k, j].start()
 
@@ -506,7 +506,6 @@
         )[0:8]
     ref_copies[0].start()
     forward(0)
-    start_first(2)
     multiply(3)
     ref_next(0)
     last_pass(0)

time: 61.3 us -> 63.7 us (1.039)
  Pallas kernels: 59.8 us -> 62.2 us
    pallas_call x1, Pallas kernels: 58.1 us -> 60.6 us  [paired_shards(): pl.pallas_call(gram_kernel, out_shape=(jax.ShapeDtypeStruct((2, width, 12...]
where the time goes in v9:
time: 63.7 us; the launch traced here: 63.5 us
  Pallas kernels  62.2 us (98%)
  local copies, waits for them, and re-layouts  0.65 us (1%)
  between operations  0.65 us (1%)
    pallas_call x1, Pallas kernels, paired_shards(): pl.pallas_call(gram_kernel, out_shape=(jax.ShapeDtypeStruct((2, width, 12...  60.6 us
    pallas_call x1, Pallas kernels, paired_shards(): pl.pallas_call(functools.partial(finish_kernel, pixel_scale), out_shape=(...  1.64 us

profile of v9, /device:TPU:0, one launch (start us, length us, event | category | flops | bytes accessed | tf_op | source)
XLA Modules:
  0.0 63.5 jit_solution(14843432810261241276)
XLA Ops:
  0.6 0.0 copy-start
  0.6 0.6 %copy-done = s32[64]{0:T(128)S(1)} copy-done((s32[64]{0:T(128)S(1)}, s32[64]{0:T(128)}, u32[]{:S(2)}) %copy-start) | copy-done | bytes 280
  1.3 60.6 %shard_map.41 = (f32[2,1024,128]{2,1,0:T(8,128)S(1)}, f32[2,8,1024]{2,1,0:T(8,128)S(1)}) custom-call(bf16[4,512,1024]{2,1,0:T(8,128)(2,1)} %frames_hbm.1, s32[1,64]{1,0:T(1,128)S(1)} %bitcast.3), custom_call_target="tpu_custom_call" | custom-call | tf_op jit(solution)/shard_map/pallas_call | solution.py:635
  61.9 1.6 %shard_map.42 = (f32[2,64,1024]{2,1,0:T(8,128)}, f32[2,64,1024]{2,1,0:T(8,128)}) custom-call(f32[2,1024,128]{2,1,0:T(8,128)S(1)} %get-tuple-element.6.gram_ref, f32[2,8,1024]{2,1,0:T(8,128)S(1)} %get-tuple-element.7.sums_ref), custom_call_target="tpu_custom_call" | custom-call | tf_op jit(solution)/shard_map/pallas_call | solution.py:687
Async XLA Ops:
  0.6 0.7 %copy-start = (s32[64]{0:T(128)S(1)}, s32[64]{0:T(128)}, u32[]{:S(2)}) copy-start(s32[64]{0:T(128)} %param.3) | copy-start | bytes 772
